TPU v7x, 32 devices: a whole 2x2x4 slice. The times are simulated.
32 devices in a mesh: grp: 2 (over x), own: 16 (over z, y, core).
Axes of the slice: x: 2, y: 2, z: 4, core: 2. Of those that a mesh axis runs over, the one named last changes fastest.
Arguments:
- left: bfloat16 [2048, 128, 64], P(('grp', 'own')), may hold values from -0.75 to 0.75
- right: bfloat16 [2048, 128, 64], P(('grp', 'own')), may hold values from -0.75 to 0.75
- values: bfloat16 [2048, 128], P(('grp', 'own')), may hold values from -6 to 6
- core: bfloat16 [10240, 64, 64], P(('grp', 'own')), may hold values from -6 to 6
- tile_slice: int32 [2048], P(('grp', 'own')), may hold values from 0 to 10239, as said below
- tile_fill: int32 [2048], P(('grp', 'own')), may hold values from 64 to 128
Outputs:
- new_core: bfloat16 [10240, 64, 64], P(('grp', 'own'))
- new_left: bfloat16 [2048, 128, 64], P(('grp', 'own'))
Inputs may be any that keep to these rules, and one draw needn't show every extreme that they name: `tile_slice`: call j // 320 the block of slice j and its remainder mod 16 its class. Among the tiles of one device at most 8 have slices of one class; in every group of 16 consecutive devices some class gets exactly 8 tiles from every device of the group.
All inputs are finite; a program needn't handle non-finite values.
Results may differ from a plain program's by a relative error of at most 0.0052.
Values may be sent and summed in bfloat16 or wider, within the bound.
A program may use at most 128 MiB of HBM per device.

v0:
```python
import jax
import jax.numpy as jnp
from jax import lax
from jax.sharding import PartitionSpec as P


def tile_terms(left_tiles, right_tiles, value_tiles, fill_counts, slice_tables):
    tile_rows = left_tiles.shape[1]
    projected = jnp.einsum(
        "sea,sab->seb", left_tiles, slice_tables, preferred_element_type=jnp.float32
    )
    predicted = jnp.sum(projected * right_tiles.astype(jnp.float32), axis=-1)
    live_rows = jnp.arange(tile_rows)[None, :] < fill_counts[:, None]
    residual = jnp.where(live_rows, predicted - value_tiles.astype(jnp.float32), 0.0)
    weighted = (residual[:, :, None] * left_tiles.astype(jnp.float32)).astype(jnp.bfloat16)
    return jnp.einsum("sea,seb->sab", weighted, right_tiles, preferred_element_type=jnp.float32)


def body(left, right, values, core, tile_slice, tile_fill):
    owners = lax.axis_size("own")
    groups = lax.axis_size("grp")
    tile_count, tile_rows, rank_width = left.shape
    per_device = core.shape[0]
    local_count = groups * per_device
    slot_cap = 2 * tile_count // owners
    slot_total = owners * slot_cap
    dev_block = tile_slice // per_device
    target_owner = dev_block % owners
    local_slice = dev_block // owners * per_device + tile_slice % per_device
    positions = jnp.arange(tile_count)
    same_owner = target_owner[:, None] == target_owner[None, :]
    earlier = positions[None, :] < positions[:, None]
    rank_among = jnp.sum((same_owner & earlier).astype(jnp.int32), axis=1)
    slot_of_tile = target_owner * slot_cap + rank_among
    slot_match = slot_of_tile[None, :] == jnp.arange(slot_total)[:, None]
    slot_live = jnp.any(slot_match, axis=1)
    tile_of_slot = jnp.sum(jnp.where(slot_match, positions[None, :], 0), axis=1)
    send_slice = jnp.where(slot_live, local_slice[tile_of_slot], 0)
    old_tables = lax.all_gather(core, "grp", axis=0, tiled=True)
    send_left = left[tile_of_slot]
    send_right = right[tile_of_slot]
    send_values = values[tile_of_slot]
    send_fill = jnp.where(slot_live, tile_fill[tile_of_slot], 0)
    got_left, got_right, got_values, got_slice, got_fill = (
        lax.all_to_all(send_left, "own", split_axis=0, concat_axis=0, tiled=True),
        lax.all_to_all(send_right, "own", split_axis=0, concat_axis=0, tiled=True),
        lax.all_to_all(send_values, "own", split_axis=0, concat_axis=0, tiled=True),
        lax.all_to_all(send_slice, "own", split_axis=0, concat_axis=0, tiled=True),
        lax.all_to_all(send_fill, "own", split_axis=0, concat_axis=0, tiled=True),
    )
    tile_grad = tile_terms(got_left, got_right, got_values, got_fill, old_tables[got_slice])
    selector = (got_slice[:, None] == jnp.arange(local_count)[None, :]).astype(jnp.float32)
    grad_part = jnp.dot(
        selector.T,
        tile_grad.reshape(slot_total, rank_width * rank_width),
        precision=lax.Precision.HIGHEST,
        preferred_element_type=jnp.float32,
    ).reshape(local_count, rank_width, rank_width)
    grad_whole = lax.psum(grad_part, "grp")
    new_tables = (old_tables.astype(jnp.float32) - grad_whole).astype(jnp.bfloat16)
    new_mine = lax.dynamic_slice_in_dim(
        new_tables, lax.axis_index("grp") * per_device, per_device, 0
    )
    refreshed = jnp.einsum(
        "sea,sab->seb", got_left, new_tables[got_slice], preferred_element_type=jnp.float32
    ).astype(jnp.bfloat16)
    returned = lax.all_to_all(refreshed, "own", split_axis=0, concat_axis=0, tiled=True)
    new_left = returned[slot_of_tile]
    return (new_mine, new_left)


def solution(mesh):
    return jax.shard_map(
        body,
        mesh=mesh,
        in_specs=(
            P(("grp", "own"), None, None),
            P(("grp", "own"), None, None),
            P(("grp", "own"), None),
            P(("grp", "own"), None, None),
            P(("grp", "own")),
            P(("grp", "own")),
        ),
        out_specs=(P(("grp", "own"), None, None), P(("grp", "own"), None, None)),
        check_vma=False,
    )
```

profile of v0, /device:TPU:13, one launch (start us, length us, event | category | flops | bytes accessed | tf_op | source)
XLA Modules:
  0.0 553.7 jit_solution(16343435588163778203)
XLA Ops:
  7.2 0.0 copy-start
  7.2 0.8 fusion.10
  8.0 0.2 convert_reduce_fusion
  8.2 0.1 select_reduce_fusion
  8.2 0.1 fusion.8
  8.4 1.2 gather_fusion
  9.6 1.6 gather_fusion.1
  11.2 0.7 select_n.96
  11.9 6.6 %all-to-all-start = ((s32[16,8,1]{1,2,0:T(1,128)}), s32[16,8,1]{1,2,0:T(1,128)S(1)}, u32[]{:S(2)}, u32[]{:S(2)}) async-start(s32[16,8,1]{1,2,0:T(1,128)} %bitcast.2), calls=%async_computation | async-start | bytes 16384 | tf_op jit(solution)/shard_map/all_to_all | solution.py:48
  18.5 0.7 select_n.98
  19.1 3.0 all-to-all-done
  22.2 5.9 %all-to-all-start.1 = ((s32[16,8,1]{1,2,0:T(1,128)}), s32[16,8,1]{1,2,0:T(1,128)S(1)}, u32[]{:S(2)}, u32[]{:S(2)}) async-start(s32[16,8,1]{1,2,0:T(1,128)} %bitcast.4), calls=%async_computation.1 | async-start | bytes 16384 | tf_op jit(solution)/shard_map/all_to_all | solution.py:49
  28.1 0.0 copy-done
  28.1 2.1 gather_fusion.4
  30.3 1.7 all-to-all-done.1
  32.0 6.2 %all-to-all-start.3 = ((bf16[128,128,64]{1,2,0:T(8,128)(2,1)}), bf16[128,128,64]{1,2,0:T(8,128)(2,1)S(1)}, u32[]{:S(2)}, u32[]{:S(2)}) async-start(bf16[128,128,64]{1,2,0:T(8,128)(2,1)} %gather_fusion.4), calls=%async_computation.3 | async-start | bytes 4194304 | tf_op jit(solution)/shard_map/all_to_all | solution.py:46
  38.2 0.0 all-gather.2.cloned.1.call-start
  38.2 10.1 %copy.22 = bf16[320,64,64]{2,1,0:T(8,128)(2,1)} copy(bf16[320,64,64]{0,2,1:T(8,128)(2,1)} %param.9) | data formatting | bytes 5242880 | tf_op args[3]
  48.3 0.0 copy-start.3
  48.3 0.0 all-gather.2.cloned.1.call-update
  48.3 1.2 copy-done.3
  49.5 2.1 gather_fusion.2
  51.6 0.0 copy-start.4
  51.6 34.4 %all-to-all-done.3 = bf16[128,128,64]{1,2,0:T(8,128)(2,1)S(1)} async-done(((bf16[128,128,64]{1,2,0:T(8,128)(2,1)}), bf16[128,128,64]{1,2,0:T(8,128)(2,1)S(1)}, u32[]{:S(2)}, u32[]{:S(2)}) %all-to-all-start.3) | async-done | bytes 2097184 | tf_op jit(solution)/shard_map/all_to_all | solution.py:46
  86.0 0.0 copy-start.2
  86.0 1.3 copy-done.2
  87.4 4.5 all-to-all-start.2
  91.8 0.0 copy-done.4
  91.8 1.3 gather_fusion.5
  93.2 0.1 all_to_all.28
  93.2 0.5 broadcast.127
  93.8 0.7 reduce.9
  94.4 0.1 eq.50
  94.5 0.7 reduce.8
  95.2 0.1 lt.81
  95.3 83.3 %all-gather.2.cloned.1.call-done = bf16[640,64,64]{2,1,0:T(8,128)(2,1)} async-done(((bf16[320,64,64]{2,1,0:T(8,128)(2,1)}), bf16[640,64,64]{2,1,0:T(8,128)(2,1)}) %all-gather.2.cloned.1.call-update) | async-done | bytes 5242896 | tf_op jit(solution)/shard_map/all_gather | solution.py:39
  178.6 6.1 %gather_fusion.3 = bf16[128,64,64]{2,1,0:T(8,128)(2,1)} fusion(bf16[640,64,64]{2,1,0:T(8,128)(2,1)} %all-gather.2.cloned.1.call-done, s32[1024]{0:T(1024)S(1)} %pad_clamp_fusion.1), kind=kCustom, calls=%fused_computation.3 | custom fusion | bytes 2097664 | tf_op jit(solution)/shard_map/gather | solution.py:51
  184.7 0.0 all-to-all-done.2
  184.7 6.4 %all-to-all-start.4 = ((bf16[16,8,128]{2,1,0:T(8,128)(2,1)}), bf16[16,8,128]{2,1,0:T(8,128)(2,1)S(1)}, u32[]{:S(2)}, u32[]{:S(2)}) async-start(bf16[16,8,128]{2,1,0:T(8,128)(2,1)} %bitcast.6), calls=%async_computation.4 | async-start | bytes 65536 | tf_op jit(solution)/shard_map/all_to_all | solution.py:47
  191.1 0.2 all-reduce.2.cloned.1.call-start
  191.3 3.2 multiply_reduce_fusion
  194.6 0.7 all-to-all-done.4
  195.3 0.1 fusion.7
  195.4 4.9 fusion
  200.2 4.8 copy.27
  205.0 8.9 %fusion.1 = f32[640,64,64]{0,2,1:T(8,128)} fusion(f32[128,64,64]{0,2,1:T(8,128)} %copy.27, s32[128]{0:T(128)S(1)} %eq.50), kind=kOutput, calls=%fused_computation.12 | convolution fusion | flops 4026613760 | bytes 12583424 | tf_op jit(solution)/shard_map/dot_general | solution.py:53
  213.9 0.0 all-reduce.2.cloned.1.call-update
  213.9 14.3 %copy.23 = bf16[640,64,64]{0,2,1:T(8,128)(2,1)} copy(bf16[640,64,64]{2,1,0:T(8,128)(2,1)} %all-gather.2.cloned.1.call-done) | data formatting | bytes 10485760 | tf_op jit(solution)/shard_map/all_gather | solution.py:39
  228.2 228.0 %all-reduce.2.cloned.1.call-done = f32[640,64,64]{0,2,1:T(8,128)} async-done(((f32[640,64,64]{0,2,1:T(8,128)}), f32[640,64,64]{0,2,1:T(8,128)}) %all-reduce.2.cloned.1.call-update) | async-done | bytes 10485776 | tf_op jit(solution)/shard_map/psum | solution.py:59
  456.2 9.6 %subtract_convert_fusion = bf16[640,64,64]{0,2,1:T(8,128)(2,1)} fusion(f32[640,64,64]{0,2,1:T(8,128)} %all-reduce.2.cloned.1.call-done, bf16[640,64,64]{0,2,1:T(8,128)(2,1)} %copy.23), kind=kLoop, calls=%fused_computation.8 | loop fusion | flops 7864320 | bytes 20971520 | tf_op jit(solution)/shard_map/convert_element_type | solution.py:60
  465.8 15.7 %copy.28 = bf16[640,64,64]{2,1,0:T(8,128)(2,1)} copy(bf16[640,64,64]{0,2,1:T(8,128)(2,1)} %subtract_convert_fusion) | data formatting | bytes 10485760 | tf_op jit(solution)/shard_map/convert_element_type | solution.py:60
  481.5 6.1 %gather_fusion.6 = bf16[128,64,64]{2,1,0:T(8,128)(2,1)} fusion(bf16[640,64,64]{2,1,0:T(8,128)(2,1)} %copy.28, s32[1024]{0:T(1024)S(1)} %pad_clamp_fusion.1), kind=kCustom, calls=%fused_computation.6 | custom fusion | bytes 2097664 | tf_op jit(solution)/shard_map/gather | solution.py:65
  487.6 3.8 convolution_convert_fusion
  491.4 6.4 %all-to-all-start.5 = ((bf16[128,128,64]{1,2,0:T(8,128)(2,1)}), bf16[128,128,64]{1,2,0:T(8,128)(2,1)S(1)}, u32[]{:S(2)}, u32[]{:S(2)}) async-start(bf16[128,128,64]{1,2,0:T(8,128)(2,1)} %convolution_convert_fusion), calls=%async_computation.5 | async-start | bytes 4194304 | tf_op jit(solution)/shard_map/all_to_all | solution.py:67
  497.8 0.0 copy-start.1
  497.8 5.8 %constant_dynamic-slice_fusion = bf16[320,64,64]{0,2,1:T(8,128)(2,1)} fusion(bf16[640,64,64]{0,2,1:T(8,128)(2,1)} %subtract_convert_fusion, s32[]{:T(128)S(6)} %select_n.101), kind=kLoop, calls=%fused_computation.47 | loop fusion | bytes 5242884 | tf_op jit(solution)/shard_map/dynamic_slice | solution.py:61
  503.6 41.6 %all-to-all-done.5 = bf16[128,128,64]{1,2,0:T(8,128)(2,1)S(1)} async-done(((bf16[128,128,64]{1,2,0:T(8,128)(2,1)}), bf16[128,128,64]{1,2,0:T(8,128)(2,1)S(1)}, u32[]{:S(2)}, u32[]{:S(2)}) %all-to-all-start.5) | async-done | bytes 2097184 | tf_op jit(solution)/shard_map/all_to_all | solution.py:67
  545.2 1.6 gather_fusion.7
  546.9 0.0 copy-done.1
  (8 shorter events, 0.1 us)
Async XLA Ops:
  7.2 21.0 %copy-start = (bf16[64,128,64]{1,2,0:T(8,128)(2,1)S(1)}, bf16[64,128,64]{1,2,0:T(8,128)(2,1)}, u32[]{:S(2)}) copy-start(bf16[64,128,64]{1,2,0:T(8,128)(2,1)} %param.7) | copy-start | bytes 3145732
  11.9 10.3 %all-to-all-start = ((s32[16,8,1]{1,2,0:T(1,128)}), s32[16,8,1]{1,2,0:T(1,128)S(1)}, u32[]{:S(2)}, u32[]{:S(2)}) async-start(s32[16,8,1]{1,2,0:T(1,128)} %bitcast.2), calls=%async_computation | async-start | bytes 16384 | tf_op jit(solution)/shard_map/all_to_all | solution.py:48
  22.2 9.8 %all-to-all-start.1 = ((s32[16,8,1]{1,2,0:T(1,128)}), s32[16,8,1]{1,2,0:T(1,128)S(1)}, u32[]{:S(2)}, u32[]{:S(2)}) async-start(s32[16,8,1]{1,2,0:T(1,128)} %bitcast.4), calls=%async_computation.1 | async-start | bytes 16384 | tf_op jit(solution)/shard_map/all_to_all | solution.py:49
  32.0 54.1 %all-to-all-start.3 = ((bf16[128,128,64]{1,2,0:T(8,128)(2,1)}), bf16[128,128,64]{1,2,0:T(8,128)(2,1)S(1)}, u32[]{:S(2)}, u32[]{:S(2)}) async-start(bf16[128,128,64]{1,2,0:T(8,128)(2,1)} %gather_fusion.4), calls=%async_computation.3 | async-start | bytes 4194304 | tf_op jit(solution)/shard_map/all_to_all | solution.py:46
  38.2 140.4 %all-gather.2.cloned.1.call-start = ((), (), s32[]{:S(2)}) async-start(), calls=%async_computation.6 | async-start | bytes 15728640 | tf_op jit(solution)/shard_map/all_gather | solution.py:39
  48.3 1.2 copy-start.3
  51.6 40.2 %copy-start.4 = (bf16[64,128]{1,0:T(8,128)(2,1)S(1)}, bf16[64,128]{1,0:T(8,128)(2,1)}, u32[]{:S(2)}) copy-start(bf16[64,128]{1,0:T(8,128)(2,1)} %param.8) | copy-start | bytes 49156
  86.0 1.3 copy-start.2
  87.4 97.4 %all-to-all-start.2 = ((bf16[128,128,64]{1,2,0:T(8,128)(2,1)}), bf16[128,128,64]{1,2,0:T(8,128)(2,1)S(1)}, u32[]{:S(2)}, u32[]{:S(2)}) async-start(bf16[128,128,64]{1,2,0:T(8,128)(2,1)} %gather_fusion.2), calls=%async_computation.2 | async-start | bytes 4194304 | tf_op jit(solution)/shard_map/all_to_all | solution.py:45
  184.7 10.5 %all-to-all-start.4 = ((bf16[16,8,128]{2,1,0:T(8,128)(2,1)}), bf16[16,8,128]{2,1,0:T(8,128)(2,1)S(1)}, u32[]{:S(2)}, u32[]{:S(2)}) async-start(bf16[16,8,128]{2,1,0:T(8,128)(2,1)} %bitcast.6), calls=%async_computation.4 | async-start | bytes 65536 | tf_op jit(solution)/shard_map/all_to_all | solution.py:47
  191.1 265.1 %all-reduce.2.cloned.1.call-start = ((), (), s32[]{:S(2)}) async-start(), calls=%async_computation.7 | async-start | bytes 20971520 | tf_op jit(solution)/shard_map/psum | solution.py:59
  491.4 53.8 %all-to-all-start.5 = ((bf16[128,128,64]{1,2,0:T(8,128)(2,1)}), bf16[128,128,64]{1,2,0:T(8,128)(2,1)S(1)}, u32[]{:S(2)}, u32[]{:S(2)}) async-start(bf16[128,128,64]{1,2,0:T(8,128)(2,1)} %convolution_convert_fusion), calls=%async_computation.5 | async-start | bytes 4194304 | tf_op jit(solution)/shard_map/all_to_all | solution.py:67
  497.8 49.1 %copy-start.1 = (bf16[64,128,64]{1,2,0:T(8,128)(2,1)S(1)}, bf16[64,128,64]{1,2,0:T(8,128)(2,1)}, u32[]{:S(2)}) copy-start(bf16[64,128,64]{1,2,0:T(8,128)(2,1)} %param.7) | copy-start | bytes 3145732
Sparse Core Ops, SparseCore 0:
  48.4 130.1 all-gather.1
  214.0 242.1 all-reduce.1
where the time goes:
time: 555 us; the launch traced here: 554 us
  waiting for transfers between devices  393 us (71%)
  local copies, waits for them, and re-layouts  77.6 us (14%)
  starting transfers between devices  36.2 us (7%)
  matrix products  20.8 us (4%)
  between operations  14.2 us (3%)
  other arithmetic  12.1 us (2%)
    psum x1, waiting for transfers between devices, body(): grad_whole = lax.psum(grad_part, 'grp')  228 us
    all_gather x1, waiting for transfers between devices, body(): old_tables = lax.all_gather(core, 'grp', axis=0, tiled=True)  83.3 us
    all_to_all x1, waiting for transfers between devices, body(): lax.all_to_all(refreshed, 'own', split_axis=0, concat_axis=0, tiled=True)  41.6 us
    all_to_all x1, waiting for transfers between devices, body(): lax.all_to_all(send_right, 'own', split_axis=0, concat_axis=0, tiled=True)  34.4 us
    convert_element_type x1, local copies, waits for them, and re-layouts, body(): (old_tables.astype(jnp.float32) - grad_whole).astype(jnp.bfloat16)  15.7 us
    all_gather x1, local copies, waits for them, and re-layouts, body(): old_tables = lax.all_gather(core, 'grp', axis=0, tiled=True)  14.3 us
    unnamed x11, local copies, waits for them, and re-layouts  12.6 us
  transfers between devices with their start and end apart: 8, of which 7 were waited for; matrix products, arithmetic and copies ran while one was open for 9% of the time, Pallas kernels for 0%

commit v1 on v0

v1 whole, which is shorter than its diff:
```python
import jax
import jax.numpy as jnp
from jax import lax
from jax.sharding import PartitionSpec as P


def pack(x):
    half = x.shape[-2] // 2
    return jnp.concatenate([x[..., :half, :], x[..., half:, :]], axis=-1)


def unpack(x):
    half = x.shape[-1] // 2
    return jnp.concatenate([x[..., :half], x[..., half:]], axis=-2)


def body(left, right, values, core, tile_slice, tile_fill):
    owners = lax.axis_size("own")
    groups = lax.axis_size("grp")
    tile_count, tile_rows, rank = left.shape
    per_device = core.shape[0]
    cap = 2 * tile_count // owners
    slots = owners * cap
    grp = lax.axis_index("grp")
    block = tile_slice // per_device
    owner = block % owners
    place = block // owners * per_device + tile_slice % per_device
    pos = jnp.arange(tile_count)
    earlier = (owner[:, None] == owner[None, :]) & (pos[None, :] < pos[:, None])
    slot_of_tile = owner * cap + jnp.sum(earlier.astype(jnp.int32), axis=1)
    match = slot_of_tile[None, :] == jnp.arange(slots)[:, None]
    live = jnp.any(match, axis=1)
    tile_of_slot = jnp.sum(jnp.where(match, pos[None, :], 0), axis=1)
    want = jnp.sum(jnp.where(match, place[None, :] + 1, 0), axis=1) - 1
    table = lax.all_to_all(
        jnp.broadcast_to(want.reshape(1, owners, cap), (groups, owners, cap)).reshape(groups * owners, cap),
        ("grp", "own"), split_axis=0, concat_axis=0, tiled=True,
    ).reshape(groups, slots)

    def shifted(step):
        return (grp + step) % groups

    local = jnp.clip(table - grp * per_device, 0, per_device - 1)
    packed = pack(core)
    mine = table[grp]
    old = packed[local[grp]]
    for step in range(1, groups):
        perm = [(g, (g + step) % groups) for g in range(groups)]
        got = lax.ppermute(packed[local[shifted(step)]], "grp", perm)
        old = jnp.where((mine // per_device == shifted(-step))[:, None, None], got, old)
    slices = lax.all_to_all(old, "own", split_axis=0, concat_axis=0, tiled=True)
    tables = unpack(slices[slot_of_tile])

    projected = jnp.einsum("sea,sab->seb", left, tables, preferred_element_type=jnp.float32)
    predicted = jnp.sum(projected * right.astype(jnp.float32), axis=-1)
    live_rows = jnp.arange(tile_rows)[None, :] < tile_fill[:, None]
    residual = jnp.where(live_rows, predicted - values.astype(jnp.float32), 0.0)
    weighted = (residual[:, :, None] * left.astype(jnp.float32)).astype(jnp.bfloat16)
    grad = jnp.einsum("sea,seb->sab", weighted, right, preferred_element_type=jnp.float32).astype(jnp.bfloat16)
    send = jnp.where(live[:, None, None], pack(grad)[tile_of_slot], jnp.bfloat16(0))
    grads = lax.all_to_all(send, "own", split_axis=0, concat_axis=0, tiled=True)
    parts, places = [grads], [mine]
    for step in range(1, groups):
        perm = [(g, (g + step) % groups) for g in range(groups)]
        parts.append(lax.ppermute(grads, "grp", perm))
        places.append(table[shifted(-step)])
    flat = jnp.concatenate(parts, axis=0)
    place_of = jnp.concatenate(places, axis=0)
    pick = (mine[:, None] == place_of[None, :]).astype(jnp.bfloat16)
    total = jnp.einsum("st,tab->sab", pick, flat, preferred_element_type=jnp.float32)
    fresh = (old.astype(jnp.float32) - total).astype(jnp.bfloat16)
    back = lax.all_to_all(fresh, "own", split_axis=0, concat_axis=0, tiled=True)
    ids = grp * per_device + jnp.arange(per_device)
    pick_core = (ids[:, None] == place_of[None, :]).astype(jnp.bfloat16)
    total_core = jnp.einsum("st,tab->sab", pick_core, flat, preferred_element_type=jnp.float32)
    new_core = (core.astype(jnp.float32) - unpack(total_core)).astype(jnp.bfloat16)
    new_left = jnp.einsum(
        "sea,sab->seb", left, unpack(back[slot_of_tile]), preferred_element_type=jnp.float32
    ).astype(jnp.bfloat16)
    return new_core, new_left


def solution(mesh):
    tiles = P(("grp", "own"), None, None)
    return jax.shard_map(
        body,
        mesh=mesh,
        in_specs=(tiles, tiles, P(("grp", "own"), None), tiles, P(("grp", "own")), P(("grp", "own"))),
        out_specs=(tiles, tiles),
        check_vma=False,
    )
```

time: 555 us -> 206 us (0.37)
  waiting for transfers between devices: 393 us -> 68.9 us
  blocking collectives: 0 us -> 29.6 us
  local copies, waits for them, and re-layouts: 77.6 us -> 56.2 us
  starting transfers between devices: 36.2 us -> 21.5 us
  matrix products: 20.8 us -> 6.7 us
  between operations: 14.2 us -> 0.87 us
  other arithmetic: 12.1 us -> 20.1 us
    psum x1 -> x0, waiting for transfers between devices: 228 us -> none  [body(): grad_whole = lax.psum(grad_part, 'grp')]
    all_gather x1 -> x0, waiting for transfers between devices: 83.3 us -> none  [body(): old_tables = lax.all_gather(core, 'grp', axis=0, tiled=True)]
    all_to_all x6 -> x3, waiting for transfers between devices: 81.4 us -> 24.8 us  [the longest x1 24.8 us: body(): slices = lax.all_to_all(old, 'own', split_axis=0, concat_axis=0, tiled=True)]
    ppermute x0 -> x2, waiting for transfers between devices: none -> 44.1 us  [the longest x1 23.4 us: body(): parts.append(lax.ppermute(grads, 'grp', perm))]
    all_to_all x0 -> x1, blocking collectives: none -> 29.6 us  [body(): grads = lax.all_to_all(send, 'own', split_axis=0, concat_axis=0, tiled=True)]
    unnamed x11 -> x24, local copies, waits for them, and re-layouts: 12.6 us -> 32.2 us
    all_to_all x6 -> x3, starting transfers between devices: 36 us -> 19 us  [the longest x1 6.92 us: body(): slices = lax.all_to_all(old, 'own', split_axis=0, concat_axis=0, tiled=True)]
    gather x8 -> x6, local copies, waits for them, and re-layouts: 22.2 us -> 7.47 us  [the longest x2 2.91 us: body(): got = lax.ppermute(packed[local[shifted(step)]], 'grp', perm)]
  transfers between devices with their start and end apart: 8 -> 5, of which waited for: 7 -> 3; matrix products, arithmetic and copies ran while one was open for 9% -> 25% of each run, Pallas kernels for 0% -> 0%
where the time goes in v1:
time: 206 us; the launch traced here: 204 us
  waiting for transfers between devices  68.9 us (33%)
  local copies, waits for them, and re-layouts  56.2 us (27%)
  blocking collectives  29.6 us (14%)
  starting transfers between devices  21.5 us (10%)
  other arithmetic  20.1 us (10%)
  matrix products  6.7 us (3%)
    unnamed x24, local copies, waits for them, and re-layouts  32.2 us
    all_to_all x1, blocking collectives, body(): grads = lax.all_to_all(send, 'own', split_axis=0, concat_axis=0, tiled=True)  29.6 us
    all_to_all x1, waiting for transfers between devices, body(): slices = lax.all_to_all(old, 'own', split_axis=0, concat_axis=0, tiled=True)  24.8 us
    ppermute x1, waiting for transfers between devices, body(): parts.append(lax.ppermute(grads, 'grp', perm))  23.4 us
    ppermute x1, waiting for transfers between devices, body(): got = lax.ppermute(packed[local[shifted(step)]], 'grp', perm)  20.7 us
    convert_element_type x1, other arithmetic, body(): (core.astype(jnp.float32) - unpack(total_core)).astype(jnp.bfloat16)  9.59 us
    slice x3, local copies, waits for them, and re-layouts, unpack(): return jnp.concatenate([x[..., :half], x[..., half:]], axis=-2)  7.97 us
    all_to_all x1, starting transfers between devices, body(): slices = lax.all_to_all(old, 'own', split_axis=0, concat_axis=0, tiled=True)  6.92 us
  transfers between devices with their start and end apart: 5, of which 3 were waited for; matrix products, arithmetic and copies ran while one was open for 25% of the time, Pallas kernels for 0%

profile of v1, /device:TPU:13, one launch (start us, length us, event | category | flops | bytes accessed | tf_op | source)
XLA Modules:
  0.0 203.8 jit_solution(15944255243779529812)
XLA Ops:
  0.6 0.7 fusion.33
  1.3 0.2 convert_reduce_fusion
  1.5 0.1 select_reduce_fusion
  1.6 0.1 sub.40
  1.7 0.6 broadcast_in_dim.72
  2.3 6.3 %all-to-all-start = ((s32[32,1,8]{2,1,0:T(1,128)}), s32[32,1,8]{2,1,0:T(1,128)S(1)}, u32[]{:S(2)}, u32[]{:S(2)}) async-start(s32[32,1,8]{2,1,0:T(1,128)} %bitcast), calls=%async_computation | async-start | bytes 32768 | tf_op jit(solution)/shard_map/all_to_all | solution.py:35
  8.6 3.9 %fusion.40 = (bf16[320,32,64]{0,2,1:T(8,128)(2,1)}, bf16[320,32,64]{0,2,1:T(8,128)(2,1)}) fusion(bf16[320,64,64]{0,2,1:T(8,128)(2,1)} %param.9), kind=kLoop, calls=%fused_computation.85 | loop fusion | bytes 5242880 | tf_op jit(solution)/shard_map/slice | solution.py:9
  12.5 5.6 %copy.53 = bf16[320,32,64]{2,1,0:T(8,128)(2,1)S(1)} copy(bf16[320,32,64]{0,2,1:T(8,128)(2,1)} %get-tuple-element.20) | data formatting | bytes 2621440
  18.1 5.9 %copy.54 = bf16[320,32,64]{2,1,0:T(8,128)(2,1)} copy(bf16[320,32,64]{0,2,1:T(8,128)(2,1)} %get-tuple-element.21) | data formatting | bytes 2621440
  24.0 4.7 %pad_maximum_fusion = bf16[320,32,128]{2,1,0:T(8,128)(2,1)} fusion(bf16[320,32,64]{2,1,0:T(8,128)(2,1)} %copy.54, bf16[320,32,64]{2,1,0:T(8,128)(2,1)S(1)} %copy.53), kind=kLoop, calls=%fused_computation.7 | loop fusion | flops 5242880 | bytes 5242880 | tf_op jit(solution)/shard_map/concatenate | solution.py:9
  28.7 0.0 all-to-all-done
  28.7 0.5 broadcast.139
  29.2 0.7 reduce.3
  29.9 0.1 reshape.122
  30.0 2.5 %gather_fusion = bf16[128,32,128]{2,1,0:T(8,128)(2,1)S(1)} fusion(bf16[320,32,128]{2,1,0:T(8,128)(2,1)} %pad_maximum_fusion, s32[1024]{0:T(1024)S(1)} %pad_clamp_fusion.3), kind=kCustom, calls=%fused_computation | custom fusion | bytes 2097664 | tf_op jit(solution)/shard_map/gather | solution.py:49
  32.5 0.4 copy.42
  32.9 1.2 collective-permute-start
  34.2 2.5 %gather_fusion.1 = bf16[128,32,128]{2,1,0:T(8,128)(2,1)S(1)} fusion(bf16[320,32,128]{2,1,0:T(8,128)(2,1)} %pad_maximum_fusion, s32[1024]{0:T(1024)S(1)} %pad_clamp_fusion.2), kind=kCustom, calls=%fused_computation.1 | custom fusion | bytes 2097664 | tf_op jit(solution)/shard_map/gather | solution.py:46
  36.7 20.7 %collective-permute-done = bf16[128,32,128]{2,0,1:T(8,128)(2,1)S(1)} collective-permute-done((bf16[128,32,128]{2,0,1:T(8,128)(2,1)S(1)}, bf16[128,32,128]{2,0,1:T(8,128)(2,1)S(1)}, u32[]{:S(2)}, u32[]{:S(2)}) %collective-permute-start) | collective-permute-done | bytes 1048608 | tf_op jit(solution)/shard_map/ppermute | solution.py:49
  57.4 0.0 copy-start.5
  57.4 1.0 copy-done.5
  58.4 1.7 copy_select_fusion
  60.1 1.6 copy.44
  61.7 6.9 %all-to-all-start.1 = ((bf16[128,32,128]{2,1,0:T(8,128)(2,1)}), bf16[128,32,128]{2,1,0:T(8,128)(2,1)S(1)}, u32[]{:S(2)}, u32[]{:S(2)}) async-start(bf16[128,32,128]{2,1,0:T(8,128)(2,1)} %copy.44), calls=%async_computation.1 | async-start | bytes 2097152 | tf_op jit(solution)/shard_map/all_to_all | solution.py:51
  68.7 0.1 fusion.24
  68.8 24.8 %all-to-all-done.1 = bf16[128,32,128]{2,1,0:T(8,128)(2,1)S(1)} async-done(((bf16[128,32,128]{2,1,0:T(8,128)(2,1)}), bf16[128,32,128]{2,1,0:T(8,128)(2,1)S(1)}, u32[]{:S(2)}, u32[]{:S(2)}) %all-to-all-start.1) | async-done | bytes 1048608 | tf_op jit(solution)/shard_map/all_to_all | solution.py:51
  93.5 0.7 gather_fusion.2
  94.2 0.0 copy-start
  94.2 1.2 fusion.43
  95.4 2.5 %copy.55 = bf16[64,32,64]{1,2,0:T(8,128)(2,1)} copy(bf16[64,32,64]{2,1,0:T(8,128)(2,1)} %get-tuple-element.26) | data formatting | bytes 524288
  97.8 2.4 %copy.56 = bf16[64,32,64]{1,2,0:T(8,128)(2,1)} copy(bf16[64,32,64]{2,1,0:T(8,128)(2,1)} %get-tuple-element.27) | data formatting | bytes 524288
  100.2 0.0 copy-done
  100.2 0.0 copy-done.2
  100.2 2.5 %fusion.1 = f32[64,128]{1,0:T(8,128)S(1)} fusion(bf16[64,128,64]{1,2,0:T(8,128)(2,1)S(1)} %copy-done.2, bf16[64,128,64]{1,2,0:T(8,128)(2,1)S(1)} %copy-done, bf16[64,32,64]{1,2,0:T(8,128)(2,1)} %copy.56, bf16[64,32,64]{1,2,0:T(8,128)(2,1)} %copy.55), kind=kOutput, calls=%fused_computation.10 | convolution fusion | flops 69722112 | bytes 2654208 | tf_op jit(solution)/shard_map/sea,sab->seb/dot_general | solution.py:54
  102.7 0.0 copy-done.6
  102.7 0.0 copy-done.7
  102.7 0.1 subtract_select_fusion
  102.8 0.0 copy-done.3
  102.8 0.7 convolution_convert_fusion.1
  103.5 0.1 fusion.41
  103.6 0.3 pad_maximum_fusion.2
  103.9 0.8 gather_fusion.3
  104.6 0.2 broadcast_select_fusion
  104.8 29.6 %all_to_all.24 = bf16[128,32,128]{2,1,0:T(8,128)(2,1)S(1)} all-to-all(bf16[128,32,128]{2,1,0:T(8,128)(2,1)S(1)} %broadcast_select_fusion), channel_id=1, replica_groups=mesh['grp'=2,'own'=16] {'own'}, dimensions={0} | all-to-all | bytes 2097152 | tf_op jit(solution)/shard_map/all_to_all | solution.py:61
  134.4 1.2 collective-permute-start.1
  135.6 0.0 copy-done.4
  135.6 23.4 %collective-permute-done.1 = bf16[128,32,128]{2,1,0:T(8,128)(2,1)} collective-permute-done((bf16[128,32,128]{2,1,0:T(8,128)(2,1)S(1)}, bf16[128,32,128]{2,1,0:T(8,128)(2,1)}, u32[]{:S(2)}, u32[]{:S(2)}) %collective-permute-start.1) | collective-permute-done | bytes 1048608 | tf_op jit(solution)/shard_map/ppermute | solution.py:65
  159.1 1.7 pad_maximum_fusion.1
  160.8 0.9 subtract_convert_fusion
  161.7 1.6 copy.49
  163.4 5.8 %all-to-all-start.3 = ((bf16[128,32,128]{2,1,0:T(8,128)(2,1)}), bf16[128,32,128]{2,1,0:T(8,128)(2,1)S(1)}, u32[]{:S(2)}, u32[]{:S(2)}) async-start(bf16[128,32,128]{2,1,0:T(8,128)(2,1)} %copy.49), calls=%async_computation.3 | async-start | bytes 2097152 | tf_op jit(solution)/shard_map/all_to_all | solution.py:72
  169.2 6.3 %copy.39 = bf16[320,64,64]{2,0,1:T(8,128)(2,1)} copy(bf16[320,64,64]{0,2,1:T(8,128)(2,1)} %param.9) | data formatting | bytes 5242880 | tf_op args[3]
  175.5 1.0 fusion.4
  176.5 5.8 %fusion.39 = (f32[320,32,64]{2,0,1:T(8,128)}, f32[320,32,64]{2,0,1:T(8,128)}) fusion(f32[320,32,128]{2,0,1:T(8,128)S(1)} %fusion.4), kind=kLoop, calls=%fused_computation.84 | loop fusion | bytes 10485760 | tf_op jit(solution)/shard_map/slice | solution.py:14
  182.3 9.6 %fusion = bf16[320,64,64]{2,0,1:T(8,128)(2,1)} fusion(f32[320,32,64]{2,0,1:T(8,128)} %get-tuple-element.19, f32[320,32,64]{2,0,1:T(8,128)} %get-tuple-element.18, bf16[320,64,64]{2,0,1:T(8,128)(2,1)} %copy.39), kind=kLoop, calls=%fused_computation.6 | loop fusion | flops 5242880 | bytes 10485760 | tf_op jit(solution)/shard_map/convert_element_type | solution.py:76
  191.9 6.6 %copy.52 = bf16[320,64,64]{0,2,1:T(8,128)(2,1)} copy(bf16[320,64,64]{2,0,1:T(8,128)(2,1)} %fusion) | data formatting | bytes 5242880
  198.5 0.0 all-to-all-done.3
  198.5 0.7 gather_fusion.4
  199.1 0.0 copy-start.1
  199.1 1.0 fusion.42
  200.2 0.5 copy.57
  200.6 1.5 copy.58
  202.2 0.0 copy-done.1
  202.2 1.7 fusion.8
  (18 shorter events, 0.1 us)
Async XLA Ops:
  2.3 26.3 %all-to-all-start = ((s32[32,1,8]{2,1,0:T(1,128)}), s32[32,1,8]{2,1,0:T(1,128)S(1)}, u32[]{:S(2)}, u32[]{:S(2)}) async-start(s32[32,1,8]{2,1,0:T(1,128)} %bitcast), calls=%async_computation | async-start | bytes 32768 | tf_op jit(solution)/shard_map/all_to_all | solution.py:35
  32.9 24.4 %collective-permute-start = (bf16[128,32,128]{2,0,1:T(8,128)(2,1)S(1)}, bf16[128,32,128]{2,0,1:T(8,128)(2,1)S(1)}, u32[]{:S(2)}, u32[]{:S(2)}) collective-permute-start(bf16[128,32,128]{2,0,1:T(8,128)(2,1)S(1)} %copy.42), channel_id=1, source_target_pairs={{0,16},{16,0},{1,17},{17,1},{2,18},{18,2},{3,19},{19,3},{4,20},{20... | collective-permute-start | bytes 3145736 | tf_op jit(solution)/shard_map/ppermute | solution.py:49
  57.4 1.0 copy-start.5
  61.7 31.8 %all-to-all-start.1 = ((bf16[128,32,128]{2,1,0:T(8,128)(2,1)}), bf16[128,32,128]{2,1,0:T(8,128)(2,1)S(1)}, u32[]{:S(2)}, u32[]{:S(2)}) async-start(bf16[128,32,128]{2,1,0:T(8,128)(2,1)} %copy.44), calls=%async_computation.1 | async-start | bytes 2097152 | tf_op jit(solution)/shard_map/all_to_all | solution.py:51
  94.2 6.0 %copy-start = (bf16[64,128,64]{1,2,0:T(8,128)(2,1)S(1)}, bf16[64,128,64]{1,2,0:T(8,128)(2,1)}, u32[]{:S(2)}) copy-start(bf16[64,128,64]{1,2,0:T(8,128)(2,1)} %param.6) | copy-start | bytes 3145732
  95.4 4.9 %copy-start.2 = (bf16[64,128,64]{1,2,0:T(8,128)(2,1)S(1)}, bf16[64,128,64]{1,2,0:T(8,128)(2,1)}, u32[]{:S(2)}) copy-start(bf16[64,128,64]{1,2,0:T(8,128)(2,1)} %param.7) | copy-start | bytes 3145732
  97.8 4.9 %copy-start.6 = (bf16[64,128]{1,0:T(8,128)(2,1)S(1)}, bf16[64,128]{1,0:T(8,128)(2,1)}, u32[]{:S(2)}) copy-start(bf16[64,128]{1,0:T(8,128)(2,1)} %param.8) | copy-start | bytes 49156
  97.8 4.9 %copy-start.7 = (s32[64]{0:T(128)S(1)}, s32[64]{0:T(128)}, u32[]{:S(2)}) copy-start(s32[64]{0:T(128)} %param.11) | copy-start | bytes 772
  100.2 2.6 %copy-start.3 = (bf16[64,128,64]{1,2,0:T(8,128)(2,1)S(1)}, bf16[64,128,64]{1,2,0:T(8,128)(2,1)}, u32[]{:S(2)}) copy-start(bf16[64,128,64]{1,2,0:T(8,128)(2,1)} %param.7) | copy-start | bytes 3145732
  134.4 1.2 copy-start.4
  134.4 24.7 %collective-permute-start.1 = (bf16[128,32,128]{2,1,0:T(8,128)(2,1)S(1)}, bf16[128,32,128]{2,1,0:T(8,128)(2,1)}, u32[]{:S(2)}, u32[]{:S(2)}) collective-permute-start(bf16[128,32,128]{2,1,0:T(8,128)(2,1)S(1)} %all_to_all.24), channel_id=1, source_target_pairs={{0,16},{16,0},{1,17},{17,1},{2,18},{18,2},{3,19},{19,3},{4,20},{20... | collective-permute-start | bytes 3145736 | tf_op jit(solution)/shard_map/ppermute | solution.py:65
  163.4 35.1 %all-to-all-start.3 = ((bf16[128,32,128]{2,1,0:T(8,128)(2,1)}), bf16[128,32,128]{2,1,0:T(8,128)(2,1)S(1)}, u32[]{:S(2)}, u32[]{:S(2)}) async-start(bf16[128,32,128]{2,1,0:T(8,128)(2,1)} %copy.49), calls=%async_computation.3 | async-start | bytes 2097152 | tf_op jit(solution)/shard_map/all_to_all | solution.py:72
  199.1 3.0 %copy-start.1 = (bf16[64,128,64]{1,2,0:T(8,128)(2,1)S(1)}, bf16[64,128,64]{1,2,0:T(8,128)(2,1)}, u32[]{:S(2)}) copy-start(bf16[64,128,64]{1,2,0:T(8,128)(2,1)} %param.6) | copy-start | bytes 3145732

commit v2 on v1

--- a/solution.py
+++ b/solution.py
@@ -1,6 +1,8 @@
 import jax
 import jax.numpy as jnp
 from jax import lax
+from jax.experimental import pallas as pl
+from jax.experimental.pallas import tpu as pltpu
 from jax.sharding import PartitionSpec as P
 
 
@@ -12,6 +14,73 @@
 def unpack(x):
     half = x.shape[-1] // 2
     return jnp.concatenate([x[..., :half], x[..., half:]], axis=-2)
+
+
+CHUNKS = 1
+
+
+def one_hot(places, width):
+    lanes = lax.broadcasted_iota(jnp.int32, (places.shape[0], width), 1)
+    return (places == lanes).astype(jnp.float32).astype(jnp.bfloat16)
+
+
+def fetch_kernel(place_ref, core_ref, out_ref):
+    half = out_ref.shape[0]
+    hot = one_hot(place_ref[...], core_ref.shape[2])
+
+    def step(i, carry):
+        slab = jnp.concatenate([core_ref[i], core_ref[i + half]], axis=0)
+        out_ref[i] = lax.dot_general(
+            hot, slab, (((1,), (1,)), ((), ())), preferred_element_type=jnp.float32
+        ).astype(out_ref.dtype)
+        return carry
+
+    lax.fori_loop(0, half, step, 0, unroll=2)
+
+
+def fetch(core_t, places):
+    rank, _, count = core_t.shape
+    wanted = places.shape[0]
+    return pl.pallas_call(
+        fetch_kernel,
+        out_shape=jax.ShapeDtypeStruct((rank // 2, wanted, 2 * rank), core_t.dtype),
+        compiler_params=pltpu.CompilerParams(vmem_limit_bytes=48 * 2**20),
+        cost_estimate=pl.CostEstimate(
+            flops=2 * wanted * count * rank * rank, bytes_accessed=2 * rank * rank * (count + wanted), transcendentals=0
+        ),
+    )(places, core_t)
+
+
+def apply_kernel(place_ref, core_ref, grads_ref, out_ref):
+    half = grads_ref.shape[0]
+    rank = out_ref.shape[1]
+    hot = one_hot(place_ref[...], core_ref.shape[2])
+
+    def step(i, carry):
+        total = lax.dot_general(
+            grads_ref[i], hot, (((0,), (0,)), ((), ())), preferred_element_type=jnp.float32
+        )
+        for part, row in ((0, i), (1, i + half)):
+            change = total[part * rank:(part + 1) * rank]
+            out_ref[row] = (core_ref[row].astype(jnp.float32) - change).astype(out_ref.dtype)
+        return carry
+
+    lax.fori_loop(0, half, step, 0, unroll=2)
+
+
+def apply_grads(core_t, grads, places):
+    rank, _, count = core_t.shape
+    wanted = places.shape[0]
+    return pl.pallas_call(
+        apply_kernel,
+        out_shape=jax.ShapeDtypeStruct(core_t.shape, core_t.dtype),
+        compiler_params=pltpu.CompilerParams(vmem_limit_bytes=48 * 2**20),
+        cost_estimate=pl.CostEstimate(
+            flops=2 * wanted * count * rank * rank,
+            bytes_accessed=2 * rank * rank * (2 * count + wanted),
+            transcendentals=0,
+        ),
+    )(places, core_t, grads)
 
 
 def body(left, right, values, core, tile_slice, tile_fill):
@@ -40,15 +109,24 @@
     def shifted(step):
         return (grp + step) % groups
 
-    local = jnp.clip(table - grp * per_device, 0, per_device - 1)
-    packed = pack(core)
+    core_t = jnp.transpose(core, (1, 2, 0))
+    local = table - grp * per_device
     mine = table[grp]
-    old = packed[local[grp]]
-    for step in range(1, groups):
-        perm = [(g, (g + step) % groups) for g in range(groups)]
-        got = lax.ppermute(packed[local[shifted(step)]], "grp", perm)
-        old = jnp.where((mine // per_device == shifted(-step))[:, None, None], got, old)
-    slices = lax.all_to_all(old, "own", split_axis=0, concat_axis=0, tiled=True)
+    order = [shifted(step) for step in range(groups)]
+    found = fetch(core_t, jnp.concatenate([local[g] for g in order])[:, None])
+    half = found.shape[0] // CHUNKS
+    olds, slices = [], []
+    for c in range(CHUNKS):
+        rows = jnp.transpose(found[c * half:(c + 1) * half], (1, 0, 2))
+        old = rows[:slots]
+        for step in range(1, groups):
+            perm = [(g, (g + step) % groups) for g in range(groups)]
+            got = lax.ppermute(rows[step * slots:(step + 1) * slots], "grp", perm)
+            old = old + got
+        olds.append(old)
+        slices.append(lax.all_to_all(old, "own", split_axis=0, concat_axis=0, tiled=True))
+    old = jnp.concatenate(olds, axis=1)
+    slices = jnp.concatenate(slices, axis=1)
     tables = unpack(slices[slot_of_tile])
 
     projected = jnp.einsum("sea,sab->seb", left, tables, preferred_element_type=jnp.float32)
@@ -58,22 +136,26 @@
     weighted = (residual[:, :, None] * left.astype(jnp.float32)).astype(jnp.bfloat16)
     grad = jnp.einsum("sea,seb->sab", weighted, right, preferred_element_type=jnp.float32).astype(jnp.bfloat16)
     send = jnp.where(live[:, None, None], pack(grad)[tile_of_slot], jnp.bfloat16(0))
-    grads = lax.all_to_all(send, "own", split_axis=0, concat_axis=0, tiled=True)
-    parts, places = [grads], [mine]
+    pieces, places = [], [mine]
+    for c in range(CHUNKS):
+        grads = lax.all_to_all(
+            send[:, c * half:(c + 1) * half], "own", split_axis=0, concat_axis=0, tiled=True
+        )
+        parts = [grads]
+        for step in range(1, groups):
+            perm = [(g, (g + step) % groups) for g in range(groups)]
+            parts.append(lax.ppermute(grads, "grp", perm))
+        pieces.append(jnp.concatenate(parts, axis=0))
     for step in range(1, groups):
-        perm = [(g, (g + step) % groups) for g in range(groups)]
-        parts.append(lax.ppermute(grads, "grp", perm))
         places.append(table[shifted(-step)])
-    flat = jnp.concatenate(parts, axis=0)
+    flat = jnp.concatenate(pieces, axis=1)
     place_of = jnp.concatenate(places, axis=0)
     pick = (mine[:, None] == place_of[None, :]).astype(jnp.bfloat16)
     total = jnp.einsum("st,tab->sab", pick, flat, preferred_element_type=jnp.float32)
     fresh = (old.astype(jnp.float32) - total).astype(jnp.bfloat16)
     back = lax.all_to_all(fresh, "own", split_axis=0, concat_axis=0, tiled=True)
-    ids = grp * per_device + jnp.arange(per_device)
-    pick_core = (ids[:, None] == place_of[None, :]).astype(jnp.bfloat16)
-    total_core = jnp.einsum("st,tab->sab", pick_core, flat, preferred_element_type=jnp.float32)
-    new_core = (core.astype(jnp.float32) - unpack(total_core)).astype(jnp.bfloat16)
+    new_core_t = apply_grads(core_t, jnp.transpose(flat, (1, 0, 2)), (place_of - grp * per_device)[:, None])
+    new_core = jnp.transpose(new_core_t, (2, 0, 1))
     new_left = jnp.einsum(
         "sea,sab->seb", left, unpack(back[slot_of_tile]), preferred_element_type=jnp.float32
     ).astype(jnp.bfloat16)

time: 206 us -> 188 us (0.913)
  local copies, waits for them, and re-layouts: 56.2 us -> 24.1 us
  waiting for transfers between devices: 68.9 us -> 94.4 us
  other arithmetic: 20.1 us -> 2.5 us
  Pallas kernels: 0 us -> 10.5 us
    unnamed x24 -> x20, local copies, waits for them, and re-layouts: 32.2 us -> 10.7 us
    all_to_all x1, waiting for transfers between devices: 0.01 us -> 16.9 us  [body(): back = lax.all_to_all(fresh, 'own', split_axis=0, concat_axis=0, tiled=True)]
    pallas_call x0 -> x2, Pallas kernels: none -> 10.5 us  [the longest x1 6.05 us: apply_grads(): pl.pallas_call(apply_kernel, out_shape=jax.ShapeDtypeStruct(core_t.shape,...]
    convert_element_type x1 -> x0, other arithmetic: 9.59 us -> none  [body(): (core.astype(jnp.float32) - unpack(total_core)).astype(jnp.bfloat16)]
    slice x3 -> x2, local copies, waits for them, and re-layouts: 7.97 us -> 2.17 us  [unpack(): return jnp.concatenate([x[..., :half], x[..., half:]], axis=-2)]
    gather x3 -> x0, local copies, waits for them, and re-layouts: 5.4 us -> none  [the longest x2 2.91 us: body(): got = lax.ppermute(packed[local[shifted(step)]], 'grp', perm)]
    concatenate x2 -> x1, other arithmetic: 4.98 us -> 0.29 us  [pack(): return jnp.concatenate([x[..., :half, :], x[..., half:, :]], axis=-1)]
    all_to_all x1, waiting for transfers between devices: 0.01 us -> 4.57 us  [body(): lax.all_to_all(jnp.broadcast_to(want.reshape(1, owners, cap), (groups, ow...]
  transfers between devices with their start and end apart: 5 -> 5, of which waited for: 3 -> 5; matrix products, arithmetic and copies ran while one was open for 25% -> 0% of each run, Pallas kernels for 0% -> 3%
where the time goes in v2:
time: 188 us; the launch traced here: 187 us
  waiting for transfers between devices  94.4 us (50%)
  blocking collectives  29.5 us (16%)
  local copies, waits for them, and re-layouts  24.1 us (13%)
  starting transfers between devices  20 us (11%)
  Pallas kernels  10.5 us (6%)
  matrix products  5.27 us (3%)
  other arithmetic  2.5 us (1%)
    all_to_all x1, blocking collectives, body(): lax.all_to_all(send[:, c * half:(c + 1) * half], 'own', split_axis=0, con...  29.5 us
    all_to_all x1, waiting for transfers between devices, body(): lax.all_to_all(old, 'own', split_axis=0, concat_axis=0, tiled=True)  24.8 us
    ppermute x1, waiting for transfers between devices, body(): parts.append(lax.ppermute(grads, 'grp', perm))  24.6 us
    ppermute x1, waiting for transfers between devices, body(): got = lax.ppermute(rows[step * slots:(step + 1) * slots], 'grp', perm)  23.6 us
    all_to_all x1, waiting for transfers between devices, body(): back = lax.all_to_all(fresh, 'own', split_axis=0, concat_axis=0, tiled=True)  16.9 us
    unnamed x20, local copies, waits for them, and re-layouts  10.7 us
    all_to_all x1, starting transfers between devices, body(): lax.all_to_all(old, 'own', split_axis=0, concat_axis=0, tiled=True)  7.25 us
    all_to_all x1, starting transfers between devices, body(): lax.all_to_all(jnp.broadcast_to(want.reshape(1, owners, cap), (groups, ow...  6.3 us
  transfers between devices with their start and end apart: 5, of which 5 were waited for; matrix products, arithmetic and copies ran while one was open for 0% of the time, Pallas kernels for 3%

profile of v2, /device:TPU:13, one launch (start us, length us, event | category | flops | bytes accessed | tf_op | source)
XLA Modules:
  0.0 187.2 jit_solution(18370781805220573566)
XLA Ops:
  0.6 0.7 fusion.22
  1.3 0.2 convert_reduce_fusion
  1.5 0.1 select_reduce_fusion
  1.6 0.1 sub.44
  1.7 0.6 broadcast_in_dim.63
  2.3 6.3 %all-to-all-start = ((s32[32,1,8]{2,1,0:T(1,128)}), s32[32,1,8]{2,1,0:T(1,128)S(1)}, u32[]{:S(2)}, u32[]{:S(2)}) async-start(s32[32,1,8]{2,1,0:T(1,128)} %bitcast), calls=%async_computation | async-start | bytes 32768 | tf_op jit(solution)/shard_map/all_to_all | solution.py:104
  8.7 4.6 %all-to-all-done = s32[32,1,8]{2,1,0:T(1,128)S(1)} async-done(((s32[32,1,8]{2,1,0:T(1,128)}), s32[32,1,8]{2,1,0:T(1,128)S(1)}, u32[]{:S(2)}, u32[]{:S(2)}) %all-to-all-start) | async-done | bytes 1056 | tf_op jit(solution)/shard_map/all_to_all | solution.py:104
  13.2 0.5 broadcast.79
  13.8 0.7 reduce.3
  14.5 0.1 reshape.74
  14.6 0.1 copy.41.place_ref
  14.7 0.0 copy-start
  14.7 1.9 %copy-done = bf16[320,64,64]{0,2,1:T(8,128)(2,1)S(1)} copy-done((bf16[320,64,64]{0,2,1:T(8,128)(2,1)S(1)}, bf16[320,64,64]{0,2,1:T(8,128)(2,1)}, u32[]{:S(2)}) %copy-start) | copy-done | bytes 2621464
  16.6 4.4 %shard_map.77 = bf16[32,256,128]{2,1,0:T(8,128)(2,1)S(1)} custom-call(s32[256,1]{1,0:T(8,128)S(1)} %copy.41.place_ref, bf16[64,64,320]{2,1,0:T(8,128)(2,1)S(1)} %bitcast.38), custom_call_target="tpu_custom_call" | custom-call | flops 671088640 | bytes 4718592 | tf_op jit(solution)/shard_map/pallas_call | solution.py:44
  21.0 0.1 slice.39
  21.1 0.4 collective-permute-start
  21.5 23.6 %collective-permute-done = bf16[128,32,128]{2,0,1:T(8,128)(2,1)S(1)} collective-permute-done((bf16[128,32,128]{2,0,1:T(8,128)(2,1)S(1)}, bf16[128,32,128]{2,0,1:T(8,128)(2,1)S(1)}, u32[]{:S(2)}, u32[]{:S(2)}) %collective-permute-start) | collective-permute-done | bytes 1048608 | tf_op jit(solution)/shard_map/ppermute | solution.py:124
  45.1 0.1 slice_add_fusion
  45.2 1.6 copy.42
  46.8 7.3 %all-to-all-start.1 = ((bf16[128,32,128]{2,1,0:T(8,128)(2,1)}), bf16[128,32,128]{2,1,0:T(8,128)(2,1)S(1)}, u32[]{:S(2)}, u32[]{:S(2)}) async-start(bf16[128,32,128]{2,1,0:T(8,128)(2,1)} %copy.42), calls=%async_computation.1 | async-start | bytes 2097152 | tf_op jit(solution)/shard_map/all_to_all | solution.py:127
  54.1 0.1 fusion.16
  54.2 24.8 %all-to-all-done.1 = bf16[128,32,128]{2,1,0:T(8,128)(2,1)S(1)} async-done(((bf16[128,32,128]{2,1,0:T(8,128)(2,1)}), bf16[128,32,128]{2,1,0:T(8,128)(2,1)S(1)}, u32[]{:S(2)}, u32[]{:S(2)}) %all-to-all-start.1) | async-done | bytes 1048608 | tf_op jit(solution)/shard_map/all_to_all | solution.py:127
  79.0 0.7 gather_fusion
  79.6 1.2 fusion.32
  80.8 0.0 copy-start.2
  80.8 0.0 copy-start.4
  80.8 2.5 %copy.50 = bf16[64,32,64]{1,2,0:T(8,128)(2,1)} copy(bf16[64,32,64]{2,1,0:T(8,128)(2,1)} %get-tuple-element.14) | data formatting | bytes 524288
  83.3 2.4 %copy.51 = bf16[64,32,64]{1,2,0:T(8,128)(2,1)} copy(bf16[64,32,64]{2,1,0:T(8,128)(2,1)} %get-tuple-element.15) | data formatting | bytes 524288
  85.7 0.0 copy-done.2
  85.7 0.0 copy-done.4
  85.7 0.0 copy-start.6
  85.7 0.0 copy-start.7
  85.7 0.0 copy-start.5
  85.7 2.5 %fusion = f32[64,128]{1,0:T(8,128)S(1)} fusion(bf16[64,128,64]{1,2,0:T(8,128)(2,1)S(1)} %copy-done.4, bf16[64,128,64]{1,2,0:T(8,128)(2,1)S(1)} %copy-done.2, bf16[64,32,64]{1,2,0:T(8,128)(2,1)} %copy.51, bf16[64,32,64]{1,2,0:T(8,128)(2,1)} %copy.50), kind=kOutput, calls=%fused_computation.4 | convolution fusion | flops 69722112 | bytes 2654208 | tf_op jit(solution)/shard_map/sea,sab->seb/dot_general | solution.py:132
  88.2 0.0 copy-done.6
  88.2 0.0 copy-done.7
  88.2 0.1 subtract_select_fusion
  88.3 0.0 copy-done.5
  88.3 0.7 convolution_convert_fusion.1
  89.0 0.1 fusion.30
  89.1 0.3 pad_maximum_fusion
  89.4 0.8 gather_fusion.1
  90.1 0.2 broadcast_select_fusion
  90.3 29.5 %all_to_all.24 = bf16[128,32,128]{2,1,0:T(8,128)(2,1)S(1)} all-to-all(bf16[128,32,128]{2,1,0:T(8,128)(2,1)S(1)} %broadcast_select_fusion), channel_id=1, replica_groups=mesh['grp'=2,'own'=16] {'own'}, dimensions={0} | all-to-all | bytes 2097152 | tf_op jit(solution)/shard_map/all_to_all | solution.py:141
  119.9 1.6 fusion.29
  121.5 0.3 collective-permute-start.1
  121.7 24.6 %collective-permute-done.1 = bf16[128,32,128]{2,0,1:T(8,128)(2,1)} collective-permute-done((bf16[128,32,128]{2,0,1:T(8,128)(2,1)}, bf16[128,32,128]{2,0,1:T(8,128)(2,1)}, u32[]{:S(2)}, u32[]{:S(2)}) %collective-permute-start.1) | collective-permute-done | bytes 1048608 | tf_op jit(solution)/shard_map/ppermute | solution.py:147
  146.3 1.4 constant_dynamic-update-slice_fusion
  147.7 0.5 subtract_convert_fusion
  148.2 1.6 copy.47
  149.9 5.8 %all-to-all-start.3 = ((bf16[128,32,128]{2,1,0:T(8,128)(2,1)}), bf16[128,32,128]{2,1,0:T(8,128)(2,1)}, u32[]{:S(2)}, u32[]{:S(2)}) async-start(bf16[128,32,128]{2,1,0:T(8,128)(2,1)} %copy.47), calls=%async_computation.3 | async-start | bytes 2097152 | tf_op jit(solution)/shard_map/all_to_all | solution.py:156
  155.7 0.1 copy.39
  155.9 0.0 copy-start.1
  155.9 1.9 %copy-done.1 = bf16[320,64,64]{0,2,1:T(8,128)(2,1)S(1)} copy-done((bf16[320,64,64]{0,2,1:T(8,128)(2,1)S(1)}, bf16[320,64,64]{0,2,1:T(8,128)(2,1)}, u32[]{:S(2)}) %copy-start.1) | copy-done | bytes 2621464
  157.8 6.1 %shard_map.78 = bf16[64,64,320]{2,1,0:T(8,128)(2,1)} custom-call(s32[256,1]{1,0:T(8,128)S(1)} %broadcast_subtract_fusion.place_ref, bf16[64,64,320]{2,1,0:T(8,128)(2,1)S(1)} %bitcast.39, bf16[32,256,128]{2,1,0:T(8,128)(2,1)S(1)} %bitcast.37), custom_call_target="tpu_custom_call" | custom-call | flops 671088640 | bytes 7340032 | tf_op jit(solution)/shard_map/pallas_call | solution.py:74
  163.8 16.9 %all-to-all-done.3 = bf16[128,32,128]{2,1,0:T(8,128)(2,1)} async-done(((bf16[128,32,128]{2,1,0:T(8,128)(2,1)}), bf16[128,32,128]{2,1,0:T(8,128)(2,1)}, u32[]{:S(2)}, u32[]{:S(2)}) %all-to-all-start.3) | async-done | bytes 1048608 | tf_op jit(solution)/shard_map/all_to_all | solution.py:156
  180.7 1.9 %gather_fusion.2 = bf16[64,32,128]{2,1,0:T(8,128)(2,1)S(1)} fusion(bf16[128,32,128]{2,1,0:T(8,128)(2,1)} %all-to-all-done.3, s32[1024]{0:T(1024)S(1)} %pad_clamp_fusion.1), kind=kCustom, calls=%fused_computation.2 | custom fusion | bytes 1048832 | tf_op jit(solution)/shard_map/gather | solution.py:160
  182.6 1.0 fusion.31
  183.6 0.0 copy-start.3
  183.6 0.5 copy.52
  184.1 1.5 copy.53
  185.6 0.0 copy-done.3
  185.6 1.7 fusion.1
  (13 shorter events, 0.1 us)
Async XLA Ops:
  2.3 10.9 %all-to-all-start = ((s32[32,1,8]{2,1,0:T(1,128)}), s32[32,1,8]{2,1,0:T(1,128)S(1)}, u32[]{:S(2)}, u32[]{:S(2)}) async-start(s32[32,1,8]{2,1,0:T(1,128)} %bitcast), calls=%async_computation | async-start | bytes 32768 | tf_op jit(solution)/shard_map/all_to_all | solution.py:104
  14.7 1.9 %copy-start = (bf16[320,64,64]{0,2,1:T(8,128)(2,1)S(1)}, bf16[320,64,64]{0,2,1:T(8,128)(2,1)}, u32[]{:S(2)}) copy-start(bf16[320,64,64]{0,2,1:T(8,128)(2,1)} %param.9) | copy-start | bytes 7864324
  21.1 24.0 %collective-permute-start = (bf16[128,32,128]{2,0,1:T(8,128)(2,1)S(1)}, bf16[128,32,128]{2,0,1:T(8,128)(2,1)S(1)}, u32[]{:S(2)}, u32[]{:S(2)}) collective-permute-start(bf16[128,32,128]{2,0,1:T(8,128)(2,1)S(1)} %slice.39), channel_id=1, source_target_pairs={{0,16},{16,0},{1,17},{17,1},{2,18},{18,2},{3,19},{19,3},{4,20},{20... | collective-permute-start | bytes 3145736 | tf_op jit(solution)/shard_map/ppermute | solution.py:124
  46.8 32.1 %all-to-all-start.1 = ((bf16[128,32,128]{2,1,0:T(8,128)(2,1)}), bf16[128,32,128]{2,1,0:T(8,128)(2,1)S(1)}, u32[]{:S(2)}, u32[]{:S(2)}) async-start(bf16[128,32,128]{2,1,0:T(8,128)(2,1)} %copy.42), calls=%async_computation.1 | async-start | bytes 2097152 | tf_op jit(solution)/shard_map/all_to_all | solution.py:127
  80.8 4.9 %copy-start.2 = (bf16[64,128,64]{1,2,0:T(8,128)(2,1)S(1)}, bf16[64,128,64]{1,2,0:T(8,128)(2,1)}, u32[]{:S(2)}) copy-start(bf16[64,128,64]{1,2,0:T(8,128)(2,1)} %param.6) | copy-start | bytes 3145732
  80.8 4.9 %copy-start.4 = (bf16[64,128,64]{1,2,0:T(8,128)(2,1)S(1)}, bf16[64,128,64]{1,2,0:T(8,128)(2,1)}, u32[]{:S(2)}) copy-start(bf16[64,128,64]{1,2,0:T(8,128)(2,1)} %param.7) | copy-start | bytes 3145732
  85.7 2.5 %copy-start.6 = (bf16[64,128]{1,0:T(8,128)(2,1)S(1)}, bf16[64,128]{1,0:T(8,128)(2,1)}, u32[]{:S(2)}) copy-start(bf16[64,128]{1,0:T(8,128)(2,1)} %param.8) | copy-start | bytes 49156
  85.7 2.5 %copy-start.7 = (s32[64]{0:T(128)S(1)}, s32[64]{0:T(128)}, u32[]{:S(2)}) copy-start(s32[64]{0:T(128)} %param.11) | copy-start | bytes 772
  85.7 2.6 %copy-start.5 = (bf16[64,128,64]{1,2,0:T(8,128)(2,1)S(1)}, bf16[64,128,64]{1,2,0:T(8,128)(2,1)}, u32[]{:S(2)}) copy-start(bf16[64,128,64]{1,2,0:T(8,128)(2,1)} %param.7) | copy-start | bytes 3145732
  121.5 24.9 %collective-permute-start.1 = (bf16[128,32,128]{2,0,1:T(8,128)(2,1)}, bf16[128,32,128]{2,0,1:T(8,128)(2,1)}, u32[]{:S(2)}, u32[]{:S(2)}) collective-permute-start(bf16[128,32,128]{2,0,1:T(8,128)(2,1)} %get-tuple-element.8), channel_id=1, source_target_pairs={{0,16},{16,0},{1,17},{17,1},{2,18},{18,2},{3,19},{19,3},{4,20},{20... | collective-permute-start | bytes 3145736 | tf_op jit(solution)/shard_map/ppermute | solution.py:147
  149.9 30.8 %all-to-all-start.3 = ((bf16[128,32,128]{2,1,0:T(8,128)(2,1)}), bf16[128,32,128]{2,1,0:T(8,128)(2,1)}, u32[]{:S(2)}, u32[]{:S(2)}) async-start(bf16[128,32,128]{2,1,0:T(8,128)(2,1)} %copy.47), calls=%async_computation.3 | async-start | bytes 2097152 | tf_op jit(solution)/shard_map/all_to_all | solution.py:156
  155.9 1.9 %copy-start.1 = (bf16[320,64,64]{0,2,1:T(8,128)(2,1)S(1)}, bf16[320,64,64]{0,2,1:T(8,128)(2,1)}, u32[]{:S(2)}) copy-start(bf16[320,64,64]{0,2,1:T(8,128)(2,1)} %param.9) | copy-start | bytes 7864324
  183.6 2.0 %copy-start.3 = (bf16[64,128,64]{1,2,0:T(8,128)(2,1)S(1)}, bf16[64,128,64]{1,2,0:T(8,128)(2,1)}, u32[]{:S(2)}) copy-start(bf16[64,128,64]{1,2,0:T(8,128)(2,1)} %param.6) | copy-start | bytes 3145732

commit v3 on v2

--- a/solution.py
+++ b/solution.py
@@ -16,7 +16,7 @@
     return jnp.concatenate([x[..., :half], x[..., half:]], axis=-2)
 
 
-CHUNKS = 1
+CHUNKS = 2
 
 
 def one_hot(places, width):

time: 188 us -> 181 us (0.963)
  starting transfers between devices: 20 us -> 31.7 us
  blocking collectives: 29.5 us -> 18.5 us
  waiting for transfers between devices: 94.4 us -> 85.9 us
    all_to_all x0 -> x1, waiting for transfers between devices: none -> 12.8 us  [body(): lax.all_to_all(send[:, c * half:(c + 1) * half], 'own', split_axis=0, con...]
    all_to_all x1 -> x2, waiting for transfers between devices: 24.8 us -> 13.5 us  [body(): lax.all_to_all(old, 'own', split_axis=0, concat_axis=0, tiled=True)]
    ppermute x1 -> x2, waiting for transfers between devices: 24.6 us -> 13.4 us  [body(): parts.append(lax.ppermute(grads, 'grp', perm))]
    all_to_all x1, blocking collectives: 29.5 us -> 18.5 us  [body(): lax.all_to_all(send[:, c * half:(c + 1) * half], 'own', split_axis=0, con...]
    all_to_all x1 -> x2, starting transfers between devices: 7.25 us -> 14.1 us  [body(): lax.all_to_all(old, 'own', split_axis=0, concat_axis=0, tiled=True)]
    all_to_all x0 -> x1, starting transfers between devices: none -> 4.98 us  [body(): lax.all_to_all(send[:, c * half:(c + 1) * half], 'own', split_axis=0, con...]
    ppermute x1 -> x2, waiting for transfers between devices: 23.6 us -> 25.2 us  [body(): got = lax.ppermute(rows[step * slots:(step + 1) * slots], 'grp', perm)]
    unnamed x20 -> x24, local copies, waits for them, and re-layouts: 10.7 us -> 10.2 us
  transfers between devices with their start and end apart: 5 -> 9, of which waited for: 5 -> 7; matrix products, arithmetic and copies ran while one was open for 0% -> 2% of each run, Pallas kernels for 3% -> 3%
where the time goes in v3:
time: 181 us; the launch traced here: 180 us
  waiting for transfers between devices  85.9 us (47%)
  starting transfers between devices  31.7 us (18%)
  local copies, waits for them, and re-layouts  22.3 us (12%)
  blocking collectives  18.5 us (10%)
  Pallas kernels  10.5 us (6%)
  matrix products  6.09 us (3%)
  other arithmetic  4.11 us (2%)
    ppermute x2, waiting for transfers between devices, body(): got = lax.ppermute(rows[step * slots:(step + 1) * slots], 'grp', perm)  25.2 us
    all_to_all x1, blocking collectives, body(): lax.all_to_all(send[:, c * half:(c + 1) * half], 'own', split_axis=0, con...  18.5 us
    all_to_all x1, waiting for transfers between devices, body(): back = lax.all_to_all(fresh, 'own', split_axis=0, concat_axis=0, tiled=True)  16.4 us
    all_to_all x2, starting transfers between devices, body(): lax.all_to_all(old, 'own', split_axis=0, concat_axis=0, tiled=True)  14.1 us
    all_to_all x2, waiting for transfers between devices, body(): lax.all_to_all(old, 'own', split_axis=0, concat_axis=0, tiled=True)  13.5 us
    ppermute x2, waiting for transfers between devices, body(): parts.append(lax.ppermute(grads, 'grp', perm))  13.4 us
    all_to_all x1, waiting for transfers between devices, body(): lax.all_to_all(send[:, c * half:(c + 1) * half], 'own', split_axis=0, con...  12.8 us
    unnamed x24, local copies, waits for them, and re-layouts  10.2 us
  transfers between devices with their start and end apart: 9, of which 7 were waited for; matrix products, arithmetic and copies ran while one was open for 2% of the time, Pallas kernels for 3%

profile of v3, /device:TPU:13, one launch (start us, length us, event | category | flops | bytes accessed | tf_op | source)
XLA Modules:
  0.0 180.0 jit_solution(8243707289515739108)
XLA Ops:
  0.6 0.7 fusion.21
  1.3 0.2 convert_reduce_fusion
  1.5 0.1 select_reduce_fusion
  1.6 0.1 sub.44
  1.7 0.6 broadcast_in_dim.63
  2.3 6.3 %all-to-all-start = ((s32[32,1,8]{2,1,0:T(1,128)}), s32[32,1,8]{2,1,0:T(1,128)S(1)}, u32[]{:S(2)}, u32[]{:S(2)}) async-start(s32[32,1,8]{2,1,0:T(1,128)} %bitcast), calls=%async_computation | async-start | bytes 32768 | tf_op jit(solution)/shard_map/all_to_all | solution.py:104
  8.7 4.6 %all-to-all-done = s32[32,1,8]{2,1,0:T(1,128)S(1)} async-done(((s32[32,1,8]{2,1,0:T(1,128)}), s32[32,1,8]{2,1,0:T(1,128)S(1)}, u32[]{:S(2)}, u32[]{:S(2)}) %all-to-all-start) | async-done | bytes 1056 | tf_op jit(solution)/shard_map/all_to_all | solution.py:104
  13.2 0.5 broadcast.79
  13.8 0.7 reduce.3
  14.5 0.1 reshape.74
  14.6 0.1 copy.47.place_ref
  14.7 0.0 copy-start
  14.7 1.9 %copy-done = bf16[320,64,64]{0,2,1:T(8,128)(2,1)S(1)} copy-done((bf16[320,64,64]{0,2,1:T(8,128)(2,1)S(1)}, bf16[320,64,64]{0,2,1:T(8,128)(2,1)}, u32[]{:S(2)}) %copy-start) | copy-done | bytes 2621464
  16.6 4.4 %shard_map.77 = bf16[32,256,128]{2,1,0:T(8,128)(2,1)S(1)} custom-call(s32[256,1]{1,0:T(8,128)S(1)} %copy.47.place_ref, bf16[64,64,320]{2,1,0:T(8,128)(2,1)S(1)} %bitcast.38), custom_call_target="tpu_custom_call" | custom-call | flops 671088640 | bytes 4718592 | tf_op jit(solution)/shard_map/pallas_call | solution.py:44
  21.0 0.1 slice_bitcast_fusion.1
  21.2 0.4 collective-permute-start
  21.6 12.4 %collective-permute-done = bf16[128,16,128]{2,0,1:T(8,128)(2,1)S(1)} collective-permute-done((bf16[128,16,128]{2,0,1:T(8,128)(2,1)S(1)}, bf16[128,16,128]{2,0,1:T(8,128)(2,1)S(1)}, u32[]{:S(2)}, u32[]{:S(2)}) %collective-permute-start) | collective-permute-done | bytes 524320 | tf_op jit(solution)/shard_map/ppermute | solution.py:124
  34.0 0.1 slice_add_fusion.1
  34.0 0.8 copy-done.4
  34.9 1.1 copy.48
  36.0 7.2 %all-to-all-start.1 = ((bf16[128,16,128]{2,1,0:T(8,128)(2,1)}), bf16[128,16,128]{2,1,0:T(8,128)(2,1)S(1)}, u32[]{:S(2)}, u32[]{:S(2)}) async-start(bf16[128,16,128]{2,1,0:T(8,128)(2,1)} %copy.48), calls=%async_computation.1 | async-start | bytes 1048576 | tf_op jit(solution)/shard_map/all_to_all | solution.py:127
  43.2 0.3 collective-permute-start.1
  43.5 12.9 %collective-permute-done.1 = bf16[128,16,128]{2,0,1:T(8,128)(2,1)S(1)} collective-permute-done((bf16[128,16,128]{2,0,1:T(8,128)(2,1)S(1)}, bf16[128,16,128]{2,0,1:T(8,128)(2,1)S(1)}, u32[]{:S(2)}, u32[]{:S(2)}) %collective-permute-start.1) | collective-permute-done | bytes 524320 | tf_op jit(solution)/shard_map/ppermute | solution.py:124
  56.4 0.1 slice_add_fusion
  56.5 0.8 copy-done.6
  57.3 1.1 copy.49
  58.4 6.9 %all-to-all-start.2 = ((bf16[128,16,128]{2,1,0:T(8,128)(2,1)}), bf16[128,16,128]{2,1,0:T(8,128)(2,1)S(1)}, u32[]{:S(2)}, u32[]{:S(2)}) async-start(bf16[128,16,128]{2,1,0:T(8,128)(2,1)} %copy.49), calls=%async_computation.2 | async-start | bytes 1048576 | tf_op jit(solution)/shard_map/all_to_all | solution.py:127
  65.4 0.1 fusion.15
  65.4 13.5 %all-to-all-done.2 = bf16[128,16,128]{2,1,0:T(8,128)(2,1)S(1)} async-done(((bf16[128,16,128]{2,1,0:T(8,128)(2,1)}), bf16[128,16,128]{2,1,0:T(8,128)(2,1)S(1)}, u32[]{:S(2)}, u32[]{:S(2)}) %all-to-all-start.2) | async-done | bytes 524320 | tf_op jit(solution)/shard_map/all_to_all | solution.py:127
  78.9 0.1 pad_maximum_fusion
  79.0 0.7 gather_fusion
  79.7 1.2 fusion.32
  80.8 1.7 copy.59
  82.5 2.4 %copy.60 = bf16[64,32,64]{1,2,0:T(8,128)(2,1)} copy(bf16[64,32,64]{2,1,0:T(8,128)(2,1)} %get-tuple-element.17) | data formatting | bytes 524288
  84.9 2.1 %fusion = f32[64,128]{1,0:T(8,128)S(1)} fusion(bf16[64,128,64]{1,2,0:T(8,128)(2,1)S(1)} %copy-done.3, bf16[64,128,64]{1,2,0:T(8,128)(2,1)S(1)} %copy-done.2, bf16[64,32,64]{1,2,0:T(8,128)(2,1)} %copy.60, bf16[64,32,64]{1,2,0:T(8,128)(2,1)S(1)} %copy.59), kind=kOutput, calls=%fused_computation.5 | convolution fusion | flops 69722112 | bytes 2654208 | tf_op jit(solution)/shard_map/sea,sab->seb/dot_general | solution.py:132
  87.0 0.1 subtract_select_fusion
  87.0 0.7 convolution_convert_fusion.1
  87.7 0.1 fusion.30
  87.8 0.3 pad_maximum_fusion.1
  88.1 0.8 gather_fusion.1
  88.9 0.2 broadcast_select_fusion
  89.1 1.0 fusion.29
  90.0 18.5 %all_to_all.34 = bf16[128,16,128]{2,1,0:T(8,128)(2,1)S(1)} all-to-all(bf16[128,16,128]{2,1,0:T(8,128)(2,1)S(1)} %get-tuple-element.10), channel_id=1, replica_groups=mesh['grp'=2,'own'=16] {'own'}, dimensions={0} | all-to-all | bytes 1048576 | tf_op jit(solution)/shard_map/all_to_all | solution.py:141
  108.5 5.0 %all-to-all-start.4 = ((bf16[128,16,128]{2,1,0:T(8,128)(2,1)}), bf16[128,16,128]{2,1,0:T(8,128)(2,1)S(1)}, u32[]{:S(2)}, u32[]{:S(2)}) async-start(bf16[128,16,128]{2,1,0:T(8,128)(2,1)} %get-tuple-element.11), calls=%async_computation.4 | async-start | bytes 1048576 | tf_op jit(solution)/shard_map/all_to_all | solution.py:141
  113.5 0.9 copy.53
  114.4 0.3 collective-permute-start.2
  114.7 12.8 %all-to-all-done.4 = bf16[128,16,128]{2,1,0:T(8,128)(2,1)S(1)} async-done(((bf16[128,16,128]{2,1,0:T(8,128)(2,1)}), bf16[128,16,128]{2,1,0:T(8,128)(2,1)S(1)}, u32[]{:S(2)}, u32[]{:S(2)}) %all-to-all-start.4) | async-done | bytes 524320 | tf_op jit(solution)/shard_map/all_to_all | solution.py:141
  127.5 0.1 copy.55
  127.6 0.3 collective-permute-start.3
  128.0 13.4 %collective-permute-done.3 = bf16[128,16,128]{2,0,1:T(8,128)(2,1)S(1)} collective-permute-done((bf16[128,16,128]{2,0,1:T(8,128)(2,1)S(1)}, bf16[128,16,128]{2,0,1:T(8,128)(2,1)S(1)}, u32[]{:S(2)}, u32[]{:S(2)}) %collective-permute-start.3) | collective-permute-done | bytes 524320 | tf_op jit(solution)/shard_map/ppermute | solution.py:147
  141.4 1.7 subtract_convert_fusion
  143.1 1.6 copy.56
  144.7 5.0 %all-to-all-start.5 = ((bf16[128,32,128]{2,1,0:T(8,128)(2,1)}), bf16[128,32,128]{2,1,0:T(8,128)(2,1)S(1)}, u32[]{:S(2)}, u32[]{:S(2)}) async-start(bf16[128,32,128]{2,1,0:T(8,128)(2,1)} %copy.56), calls=%async_computation.5 | async-start | bytes 2097152 | tf_op jit(solution)/shard_map/all_to_all | solution.py:156
  149.8 0.1 copy.45
  149.9 0.0 copy-start.1
  150.0 1.5 fusion.10.grads_ref
  151.5 0.7 copy-done.1
  152.1 6.1 %shard_map.78 = bf16[64,64,320]{2,1,0:T(8,128)(2,1)} custom-call(s32[256,1]{1,0:T(8,128)S(1)} %broadcast_subtract_fusion.place_ref, bf16[64,64,320]{2,1,0:T(8,128)(2,1)S(1)} %bitcast.39, bf16[32,256,128]{2,1,0:T(8,128)(2,1)S(1)} %fusion.10.grads_ref), custom_call_target="tpu_custom_call" | custom-call | flops 671088640 | bytes 7340032 | tf_op jit(solution)/shard_map/pallas_call | solution.py:74
  158.2 16.4 %all-to-all-done.5 = bf16[128,32,128]{2,1,0:T(8,128)(2,1)S(1)} async-done(((bf16[128,32,128]{2,1,0:T(8,128)(2,1)}), bf16[128,32,128]{2,1,0:T(8,128)(2,1)S(1)}, u32[]{:S(2)}, u32[]{:S(2)}) %all-to-all-start.5) | async-done | bytes 1048608 | tf_op jit(solution)/shard_map/all_to_all | solution.py:156
  174.6 0.7 gather_fusion.2
  175.3 1.0 fusion.31
  176.3 0.5 copy.61
  176.8 1.5 copy.62
  178.3 1.7 fusion.1
  (31 shorter events, 0.2 us)
Async XLA Ops:
  2.3 10.9 %all-to-all-start = ((s32[32,1,8]{2,1,0:T(1,128)}), s32[32,1,8]{2,1,0:T(1,128)S(1)}, u32[]{:S(2)}, u32[]{:S(2)}) async-start(s32[32,1,8]{2,1,0:T(1,128)} %bitcast), calls=%async_computation | async-start | bytes 32768 | tf_op jit(solution)/shard_map/all_to_all | solution.py:104
  14.7 1.9 %copy-start = (bf16[320,64,64]{0,2,1:T(8,128)(2,1)S(1)}, bf16[320,64,64]{0,2,1:T(8,128)(2,1)}, u32[]{:S(2)}) copy-start(bf16[320,64,64]{0,2,1:T(8,128)(2,1)} %param.9) | copy-start | bytes 7864324
  21.2 12.7 %collective-permute-start = (bf16[128,16,128]{2,0,1:T(8,128)(2,1)S(1)}, bf16[128,16,128]{2,0,1:T(8,128)(2,1)S(1)}, u32[]{:S(2)}, u32[]{:S(2)}) collective-permute-start(bf16[128,16,128]{2,0,1:T(8,128)(2,1)S(1)} %slice.64), channel_id=1, source_target_pairs={{0,16},{16,0},{1,17},{17,1},{2,18},{18,2},{3,19},{19,3},{4,20},{20... | collective-permute-start | bytes 1572872 | tf_op jit(solution)/shard_map/ppermute | solution.py:124
  34.0 0.8 copy-start.4
  36.0 22.4 %all-to-all-start.1 = ((bf16[128,16,128]{2,1,0:T(8,128)(2,1)}), bf16[128,16,128]{2,1,0:T(8,128)(2,1)S(1)}, u32[]{:S(2)}, u32[]{:S(2)}) async-start(bf16[128,16,128]{2,1,0:T(8,128)(2,1)} %copy.48), calls=%async_computation.1 | async-start | bytes 1048576 | tf_op jit(solution)/shard_map/all_to_all | solution.py:127
  43.2 13.2 %collective-permute-start.1 = (bf16[128,16,128]{2,0,1:T(8,128)(2,1)S(1)}, bf16[128,16,128]{2,0,1:T(8,128)(2,1)S(1)}, u32[]{:S(2)}, u32[]{:S(2)}) collective-permute-start(bf16[128,16,128]{2,0,1:T(8,128)(2,1)S(1)} %slice.67), channel_id=1, source_target_pairs={{0,16},{16,0},{1,17},{17,1},{2,18},{18,2},{3,19},{19,3},{4,20},{20... | collective-permute-start | bytes 1572872 | tf_op jit(solution)/shard_map/ppermute | solution.py:124
  56.5 0.8 copy-start.6
  58.4 20.5 %all-to-all-start.2 = ((bf16[128,16,128]{2,1,0:T(8,128)(2,1)}), bf16[128,16,128]{2,1,0:T(8,128)(2,1)S(1)}, u32[]{:S(2)}, u32[]{:S(2)}) async-start(bf16[128,16,128]{2,1,0:T(8,128)(2,1)} %copy.49), calls=%async_computation.2 | async-start | bytes 1048576 | tf_op jit(solution)/shard_map/all_to_all | solution.py:127
  80.8 4.0 %copy-start.2 = (bf16[64,128,64]{1,2,0:T(8,128)(2,1)S(1)}, bf16[64,128,64]{1,2,0:T(8,128)(2,1)}, u32[]{:S(2)}) copy-start(bf16[64,128,64]{1,2,0:T(8,128)(2,1)} %param.6) | copy-start | bytes 3145732
  80.8 4.0 %copy-start.3 = (bf16[64,128,64]{1,2,0:T(8,128)(2,1)S(1)}, bf16[64,128,64]{1,2,0:T(8,128)(2,1)}, u32[]{:S(2)}) copy-start(bf16[64,128,64]{1,2,0:T(8,128)(2,1)} %param.7) | copy-start | bytes 3145732
  84.9 2.1 %copy-start.8 = (bf16[64,128]{1,0:T(8,128)(2,1)S(1)}, bf16[64,128]{1,0:T(8,128)(2,1)}, u32[]{:S(2)}) copy-start(bf16[64,128]{1,0:T(8,128)(2,1)} %param.8) | copy-start | bytes 49156
  84.9 2.1 %copy-start.9 = (s32[64]{0:T(128)S(1)}, s32[64]{0:T(128)}, u32[]{:S(2)}) copy-start(s32[64]{0:T(128)} %param.11) | copy-start | bytes 772
  90.0 51.3 %copy-start.5 = (bf16[128,16,128]{2,0,1:T(8,128)(2,1)S(1)}, bf16[128,16,128]{2,0,1:T(8,128)(2,1)}, u32[]{:S(2)}) copy-start(bf16[128,16,128]{2,0,1:T(8,128)(2,1)} %copy-done.4) | copy-start | bytes 1572868
  90.0 51.3 %copy-start.7 = (bf16[128,16,128]{2,0,1:T(8,128)(2,1)S(1)}, bf16[128,16,128]{2,0,1:T(8,128)(2,1)}, u32[]{:S(2)}) copy-start(bf16[128,16,128]{2,0,1:T(8,128)(2,1)} %copy-done.6) | copy-start | bytes 1572868
  108.5 19.0 %all-to-all-start.4 = ((bf16[128,16,128]{2,1,0:T(8,128)(2,1)}), bf16[128,16,128]{2,1,0:T(8,128)(2,1)S(1)}, u32[]{:S(2)}, u32[]{:S(2)}) async-start(bf16[128,16,128]{2,1,0:T(8,128)(2,1)} %get-tuple-element.11), calls=%async_computation.4 | async-start | bytes 1048576 | tf_op jit(solution)/shard_map/all_to_all | solution.py:141
  114.4 13.6 %collective-permute-start.2 = (bf16[128,16,128]{2,0,1:T(8,128)(2,1)}, bf16[128,16,128]{2,0,1:T(8,128)(2,1)}, u32[]{:S(2)}, u32[]{:S(2)}) collective-permute-start(bf16[128,16,128]{2,0,1:T(8,128)(2,1)} %copy.53), channel_id=1, source_target_pairs={{0,16},{16,0},{1,17},{17,1},{2,18},{18,2},{3,19},{19,3},{4,20},{20... | collective-permute-start | bytes 1572872 | tf_op jit(solution)/shard_map/ppermute | solution.py:147
  127.6 13.7 %collective-permute-start.3 = (bf16[128,16,128]{2,0,1:T(8,128)(2,1)S(1)}, bf16[128,16,128]{2,0,1:T(8,128)(2,1)S(1)}, u32[]{:S(2)}, u32[]{:S(2)}) collective-permute-start(bf16[128,16,128]{2,0,1:T(8,128)(2,1)S(1)} %copy.55), channel_id=1, source_target_pairs={{0,16},{16,0},{1,17},{17,1},{2,18},{18,2},{3,19},{19,3},{4,20},{20... | collective-permute-start | bytes 1572872 | tf_op jit(solution)/shard_map/ppermute | solution.py:147
  144.7 29.9 %all-to-all-start.5 = ((bf16[128,32,128]{2,1,0:T(8,128)(2,1)}), bf16[128,32,128]{2,1,0:T(8,128)(2,1)S(1)}, u32[]{:S(2)}, u32[]{:S(2)}) async-start(bf16[128,32,128]{2,1,0:T(8,128)(2,1)} %copy.56), calls=%async_computation.5 | async-start | bytes 2097152 | tf_op jit(solution)/shard_map/all_to_all | solution.py:156
  149.9 2.2 %copy-start.1 = (bf16[320,64,64]{0,2,1:T(8,128)(2,1)S(1)}, bf16[320,64,64]{0,2,1:T(8,128)(2,1)}, u32[]{:S(2)}) copy-start(bf16[320,64,64]{0,2,1:T(8,128)(2,1)} %param.9) | copy-start | bytes 7864324

commit v4 on v3

--- a/solution.py
+++ b/solution.py
@@ -1,3 +1,5 @@
+import functools
+
 import jax
 import jax.numpy as jnp
 from jax import lax
@@ -14,9 +16,6 @@
 def unpack(x):
     half = x.shape[-1] // 2
     return jnp.concatenate([x[..., :half], x[..., half:]], axis=-2)
-
-
-CHUNKS = 2
 
 
 def one_hot(places, width):
@@ -81,6 +80,184 @@
             transcendentals=0,
         ),
     )(places, core_t, grads)
+
+
+MESH = pl.DeviceIdType.MESH
+
+
+def greet(groups, owners):
+    grp, own = lax.axis_index("grp"), lax.axis_index("own")
+    barrier = pltpu.get_barrier_semaphore()
+    for step in range(1, groups):
+        pl.semaphore_signal(barrier, inc=1, device_id=(lax.rem(grp + step, groups), own), device_id_type=MESH)
+
+    def hail(i, carry):
+        pl.semaphore_signal(barrier, inc=1, device_id=(grp, lax.rem(own + i + 1, owners)), device_id_type=MESH)
+        return carry
+
+    lax.fori_loop(0, owners - 1, hail, 0)
+    pl.semaphore_wait(barrier, groups + owners - 2)
+
+
+def deliver_kernel(groups, owners, rows, old, out, inbox, cross_send, cross_recv, send_sem, recv_sem):
+    grp, own = lax.axis_index("grp"), lax.axis_index("own")
+    slots = old.shape[0]
+    cap = slots // owners
+    greet(groups, owners)
+
+    def cross(step, i):
+        start = lax.rem(own + i + 1, owners) * cap
+        return pltpu.make_async_remote_copy(
+            src_ref=rows.at[pl.ds(step * slots + start, cap)],
+            dst_ref=inbox.at[step - 1, pl.ds(start, cap)],
+            send_sem=cross_send.at[step - 1, i],
+            recv_sem=cross_recv.at[step - 1, i],
+            device_id=(lax.rem(grp + step, groups), own),
+            device_id_type=MESH,
+        )
+
+    def along(i):
+        peer = lax.rem(own + i + 1, owners)
+        return pltpu.make_async_remote_copy(
+            src_ref=old.at[pl.ds(peer * cap, cap)],
+            dst_ref=out.at[pl.ds(own * cap, cap)],
+            send_sem=send_sem.at[i],
+            recv_sem=recv_sem.at[i],
+            device_id=(grp, peer),
+            device_id_type=MESH,
+        )
+
+    def launch(i, carry):
+        for step in range(1, groups):
+            cross(step, i).start()
+        return carry
+
+    def merge(i):
+        start = lax.rem(own + i + 1, owners) * cap
+        total = rows[pl.ds(start, cap)]
+        for step in range(1, groups):
+            cross(step, i).wait_recv()
+            total = total + inbox[step - 1, pl.ds(start, cap)]
+        old[pl.ds(start, cap)] = total
+        return total
+
+    def forward(i, carry):
+        merge(i)
+        along(i).start()
+        return carry
+
+    def drain(i, carry):
+        along(i).wait()
+        return carry
+
+    def drain_cross(i, carry):
+        for step in range(1, groups):
+            cross(step, i).wait_send()
+        return carry
+
+    lax.fori_loop(0, owners, launch, 0)
+    lax.fori_loop(0, owners - 1, forward, 0)
+    out[pl.ds(own * cap, cap)] = merge(owners - 1)
+    lax.fori_loop(0, owners, drain_cross, 0)
+    lax.fori_loop(0, owners - 1, drain, 0)
+
+
+def deliver(rows, groups, owners):
+    slots = rows.shape[0] // groups
+    shape = (slots,) + rows.shape[1:]
+    return pl.pallas_call(
+        functools.partial(deliver_kernel, groups, owners),
+        out_shape=[jax.ShapeDtypeStruct(shape, rows.dtype)] * 2,
+        in_specs=[pl.BlockSpec(memory_space=pltpu.VMEM)],
+        out_specs=[pl.BlockSpec(memory_space=pltpu.VMEM)] * 2,
+        scratch_shapes=[
+            pltpu.VMEM((groups - 1,) + shape, rows.dtype),
+            pltpu.SemaphoreType.DMA((groups - 1, owners)),
+            pltpu.SemaphoreType.DMA((groups - 1, owners)),
+            pltpu.SemaphoreType.DMA((owners - 1,)),
+            pltpu.SemaphoreType.DMA((owners - 1,)),
+        ],
+        compiler_params=pltpu.CompilerParams(
+            collective_id=1, has_side_effects=True, vmem_limit_bytes=48 * 2**20
+        ),
+    )(rows)
+
+
+def collect_kernel(groups, owners, send, flat, cross_send, cross_recv, send_sem, recv_sem):
+    grp, own = lax.axis_index("grp"), lax.axis_index("own")
+    slots = send.shape[0]
+    cap = slots // owners
+    greet(groups, owners)
+
+    def along(i):
+        peer = lax.rem(own + i + 1, owners)
+        return pltpu.make_async_remote_copy(
+            src_ref=send.at[pl.ds(peer * cap, cap)],
+            dst_ref=flat.at[pl.ds(own * cap, cap)],
+            send_sem=send_sem.at[i],
+            recv_sem=recv_sem.at[i],
+            device_id=(grp, peer),
+            device_id_type=MESH,
+        )
+
+    def cross(step, i):
+        start = lax.rem(own - i - 1 + owners, owners) * cap
+        return pltpu.make_async_remote_copy(
+            src_ref=flat.at[pl.ds(start, cap)],
+            dst_ref=flat.at[pl.ds(step * slots + start, cap)],
+            send_sem=cross_send.at[step - 1, i],
+            recv_sem=cross_recv.at[step - 1, i],
+            device_id=(lax.rem(grp + step, groups), own),
+            device_id_type=MESH,
+        )
+
+    def launch(i, carry):
+        along(i).start()
+        return carry
+
+    def share(i):
+        for step in range(1, groups):
+            cross(step, i).start()
+
+    def forward(i, carry):
+        along(i).wait_recv()
+        share(i)
+        return carry
+
+    def drain(i, carry):
+        along(i).wait_send()
+        return carry
+
+    def drain_cross(i, carry):
+        for step in range(1, groups):
+            cross(step, i).wait()
+        return carry
+
+    lax.fori_loop(0, owners - 1, launch, 0)
+    flat[pl.ds(own * cap, cap)] = send[pl.ds(own * cap, cap)]
+    share(owners - 1)
+    lax.fori_loop(0, owners - 1, forward, 0)
+    lax.fori_loop(0, owners - 1, drain, 0)
+    lax.fori_loop(0, owners, drain_cross, 0)
+
+
+def collect(send, groups, owners):
+    slots = send.shape[0]
+    return pl.pallas_call(
+        functools.partial(collect_kernel, groups, owners),
+        out_shape=jax.ShapeDtypeStruct((groups * slots,) + send.shape[1:], send.dtype),
+        in_specs=[pl.BlockSpec(memory_space=pltpu.VMEM)],
+        out_specs=pl.BlockSpec(memory_space=pltpu.VMEM),
+        scratch_shapes=[
+            pltpu.SemaphoreType.DMA((groups - 1, owners)),
+            pltpu.SemaphoreType.DMA((groups - 1, owners)),
+            pltpu.SemaphoreType.DMA((owners - 1,)),
+            pltpu.SemaphoreType.DMA((owners - 1,)),
+        ],
+        compiler_params=pltpu.CompilerParams(
+            collective_id=2, has_side_effects=True, vmem_limit_bytes=48 * 2**20
+        ),
+    )(send)
 
 
 def body(left, right, values, core, tile_slice, tile_fill):
@@ -114,19 +291,7 @@
     mine = table[grp]
     order = [shifted(step) for step in range(groups)]
     found = fetch(core_t, jnp.concatenate([local[g] for g in order])[:, None])
-    half = found.shape[0] // CHUNKS
-    olds, slices = [], []
-    for c in range(CHUNKS):
-        rows = jnp.transpose(found[c * half:(c + 1) * half], (1, 0, 2))
-        old = rows[:slots]
-        for step in range(1, groups):
-            perm = [(g, (g + step) % groups) for g in range(groups)]
-            got = lax.ppermute(rows[step * slots:(step + 1) * slots], "grp", perm)
-            old = old + got
-        olds.append(old)
-        slices.append(lax.all_to_all(old, "own", split_axis=0, concat_axis=0, tiled=True))
-    old = jnp.concatenate(olds, axis=1)
-    slices = jnp.concatenate(slices, axis=1)
+    old, slices = deliver(jnp.transpose(found, (1, 0, 2)), groups, owners)
     tables = unpack(slices[slot_of_tile])
 
     projected = jnp.einsum("sea,sab->seb", left, tables, preferred_element_type=jnp.float32)
@@ -136,19 +301,10 @@
     weighted = (residual[:, :, None] * left.astype(jnp.float32)).astype(jnp.bfloat16)
     grad = jnp.einsum("sea,seb->sab", weighted, right, preferred_element_type=jnp.float32).astype(jnp.bfloat16)
     send = jnp.where(live[:, None, None], pack(grad)[tile_of_slot], jnp.bfloat16(0))
-    pieces, places = [], [mine]
-    for c in range(CHUNKS):
-        grads = lax.all_to_all(
-            send[:, c * half:(c + 1) * half], "own", split_axis=0, concat_axis=0, tiled=True
-        )
-        parts = [grads]
-        for step in range(1, groups):
-            perm = [(g, (g + step) % groups) for g in range(groups)]
-            parts.append(lax.ppermute(grads, "grp", perm))
-        pieces.append(jnp.concatenate(parts, axis=0))
+    flat = collect(send, groups, owners)
+    places = [mine]
     for step in range(1, groups):
         places.append(table[shifted(-step)])
-    flat = jnp.concatenate(pieces, axis=1)
     place_of = jnp.concatenate(places, axis=0)
     pick = (mine[:, None] == place_of[None, :]).astype(jnp.bfloat16)
     total = jnp.einsum("st,tab->sab", pick, flat, preferred_element_type=jnp.float32)

time: 181 us -> 140 us (0.77)
  Pallas kernels: 10.5 us -> 79.5 us
  waiting for transfers between devices: 85.9 us -> 17.6 us
  blocking collectives: 18.5 us -> 0 us
  starting transfers between devices: 31.7 us -> 17 us
  local copies, waits for them, and re-layouts: 22.3 us -> 15.5 us
  matrix products: 6.09 us -> 3.66 us
    pallas_call x0 -> x2, Pallas kernels: none -> 69.1 us  [the longest x1 35.7 us: deliver(): pl.pallas_call(functools.partial(deliver_kernel, groups, owners), out_sha...]
    ppermute x4 -> x0, waiting for transfers between devices: 38.6 us -> none  [the longest x2 25.2 us: body(): got = lax.ppermute(rows[step * slots:(step + 1) * slots], 'grp', perm)]
    all_to_all x3 -> x0, waiting for transfers between devices: 26.3 us -> none  [the longest x2 13.5 us: body(): lax.all_to_all(old, 'own', split_axis=0, concat_axis=0, tiled=True)]
    all_to_all x3 -> x0, starting transfers between devices: 19 us -> none  [the longest x2 14.1 us: body(): lax.all_to_all(old, 'own', split_axis=0, concat_axis=0, tiled=True)]
    all_to_all x1 -> x0, blocking collectives: 18.5 us -> none  [body(): lax.all_to_all(send[:, c * half:(c + 1) * half], 'own', split_axis=0, con...]
    all_to_all x1, starting transfers between devices: 5.04 us -> 10.7 us  [body(): back = lax.all_to_all(fresh, 'own', split_axis=0, concat_axis=0, tiled=True)]
    unnamed x24 -> x16, local copies, waits for them, and re-layouts: 10.2 us -> 6.67 us
    pallas_call x0 -> x2, local copies, waits for them, and re-layouts: none -> 3.48 us  [the longest x1 2.13 us: collect(): pl.pallas_call(functools.partial(collect_kernel, groups, owners), out_sha...]
  transfers between devices with their start and end apart: 9 -> 2, of which waited for: 7 -> 2; matrix products, arithmetic and copies ran while one was open for 2% -> 2% of each run, Pallas kernels for 3% -> 4%
where the time goes in v4:
time: 140 us; the launch traced here: 139 us
  Pallas kernels  79.5 us (57%)
  waiting for transfers between devices  17.6 us (13%)
  starting transfers between devices  17 us (12%)
  local copies, waits for them, and re-layouts  15.5 us (11%)
  other arithmetic  4.65 us (3%)
  matrix products  3.66 us (3%)
    pallas_call x1, Pallas kernels, deliver(): pl.pallas_call(functools.partial(deliver_kernel, groups, owners), out_sha...  35.7 us
    pallas_call x1, Pallas kernels, collect(): pl.pallas_call(functools.partial(collect_kernel, groups, owners), out_sha...  33.3 us
    all_to_all x1, waiting for transfers between devices, body(): back = lax.all_to_all(fresh, 'own', split_axis=0, concat_axis=0, tiled=True)  13.1 us
    all_to_all x1, starting transfers between devices, body(): back = lax.all_to_all(fresh, 'own', split_axis=0, concat_axis=0, tiled=True)  10.7 us
    unnamed x16, local copies, waits for them, and re-layouts  6.67 us
    all_to_all x1, starting transfers between devices, body(): lax.all_to_all(jnp.broadcast_to(want.reshape(1, owners, cap), (groups, ow...  6.3 us
    pallas_call x1, Pallas kernels, apply_grads(): pl.pallas_call(apply_kernel, out_shape=jax.ShapeDtypeStruct(core_t.shape,...  6.05 us
    all_to_all x1, waiting for transfers between devices, body(): lax.all_to_all(jnp.broadcast_to(want.reshape(1, owners, cap), (groups, ow...  4.41 us
  transfers between devices with their start and end apart: 2, of which 2 were waited for; matrix products, arithmetic and copies ran while one was open for 2% of the time, Pallas kernels for 4%

profile of v4, /device:TPU:13, one launch (start us, length us, event | category | flops | bytes accessed | tf_op | source)
XLA Modules:
  0.0 138.9 jit_solution(5062106185188674147)
XLA Ops:
  0.6 0.7 fusion.22
  1.3 0.2 convert_reduce_fusion
  1.5 0.1 select_reduce_fusion
  1.6 0.1 sub.44
  1.7 0.6 broadcast_in_dim.63
  2.3 6.3 %all-to-all-start = ((s32[32,1,8]{2,1,0:T(1,128)}), s32[32,1,8]{2,1,0:T(1,128)S(1)}, u32[]{:S(2)}, u32[]{:S(2)}) async-start(s32[32,1,8]{2,1,0:T(1,128)} %bitcast), calls=%async_computation | async-start | bytes 32768 | tf_op jit(solution)/shard_map/all_to_all | solution.py:281
  8.7 0.1 fusion.16
  8.8 4.4 %all-to-all-done = s32[32,1,8]{2,1,0:T(1,128)S(1)} async-done(((s32[32,1,8]{2,1,0:T(1,128)}), s32[32,1,8]{2,1,0:T(1,128)S(1)}, u32[]{:S(2)}, u32[]{:S(2)}) %all-to-all-start) | async-done | bytes 1056 | tf_op jit(solution)/shard_map/all_to_all | solution.py:281
  13.2 0.5 broadcast.79
  13.8 0.7 reduce.3
  14.5 0.1 reshape.74
  14.6 0.1 copy.41.place_ref
  14.7 0.0 copy-start
  14.7 1.9 %copy-done = bf16[320,64,64]{0,2,1:T(8,128)(2,1)S(1)} copy-done((bf16[320,64,64]{0,2,1:T(8,128)(2,1)S(1)}, bf16[320,64,64]{0,2,1:T(8,128)(2,1)}, u32[]{:S(2)}) %copy-start) | copy-done | bytes 2621464
  16.6 4.4 %shard_map.77 = bf16[32,256,128]{2,1,0:T(8,128)(2,1)S(1)} custom-call(s32[256,1]{1,0:T(8,128)S(1)} %copy.41.place_ref, bf16[64,64,320]{2,1,0:T(8,128)(2,1)S(1)} %bitcast.38), custom_call_target="tpu_custom_call" | custom-call | flops 671088640 | bytes 4718592 | tf_op jit(solution)/shard_map/pallas_call | solution.py:43
  21.0 1.4 copy.57
  22.4 35.7 %shard_map.78 = (bf16[128,32,128]{2,1,0:T(8,128)(2,1)S(1)}, bf16[128,32,128]{2,1,0:T(8,128)(2,1)S(1)}) custom-call(bf16[256,32,128]{2,1,0:T(8,128)(2,1)S(1)} %bitcast.40), custom_call_target="tpu_custom_call" | custom-call | tf_op jit(solution)/shard_map/pallas_call | solution.py:168
  58.1 0.7 gather_fusion
  58.8 0.0 copy-start.3
  58.8 0.0 copy-start.5
  58.8 0.2 fusion.31
  59.0 0.0 copy-start.6
  59.0 0.0 copy-start.7
  59.1 1.0 copy-done.3
  60.0 0.3 copy-done.5
  60.3 0.6 fusion
  61.0 0.0 copy-done.6
  61.0 0.0 copy-done.7
  61.0 0.1 subtract_select_fusion
  61.1 0.7 convolution_convert_fusion.1
  61.7 0.1 fusion.29
  61.8 0.3 pad_maximum_fusion
  62.1 0.8 gather_fusion.1
  62.9 0.2 broadcast_select_fusion.send
  63.1 33.3 %shard_map.79 = bf16[256,32,128]{2,1,0:T(8,128)(2,1)S(1)} custom-call(bf16[128,32,128]{2,1,0:T(8,128)(2,1)S(1)} %broadcast_select_fusion.send), custom_call_target="tpu_custom_call" | custom-call | tf_op jit(solution)/shard_map/pallas_call | solution.py:246
  96.5 0.9 fusion.2
  97.4 2.3 %fusion.1 = bf16[128,32,128]{2,1,0:T(8,128)(2,1)} fusion(f32[128,32,128]{2,0,1:T(8,128)S(1)} %fusion.2, bf16[128,32,128]{2,1,0:T(8,128)(2,1)S(1)} %get-tuple-element.5), kind=kLoop, calls=%fused_computation.6 | loop fusion | flops 1572864 | bytes 4194304 | tf_op jit(solution)/shard_map/convert_element_type | solution.py:311
  99.6 10.7 %all-to-all-start.1 = ((bf16[128,32,128]{2,1,0:T(8,128)(2,1)}), bf16[128,32,128]{2,1,0:T(8,128)(2,1)}, u32[]{:S(2)}, u32[]{:S(2)}) async-start(bf16[128,32,128]{2,1,0:T(8,128)(2,1)} %fusion.1), calls=%async_computation.1 | async-start | bytes 2097152 | tf_op jit(solution)/shard_map/all_to_all | solution.py:312
  110.3 2.1 %copy.58 = bf16[256,32,128]{2,0,1:T(8,128)(2,1)} copy(bf16[256,32,128]{2,1,0:T(8,128)(2,1)S(1)} %shard_map.79) | data formatting | bytes 4194304 | tf_op jit(solution)/shard_map/pallas_call | solution.py:246
  112.5 0.1 copy.39
  112.6 0.0 copy-start.1
  112.7 1.9 %copy-done.1 = bf16[320,64,64]{0,2,1:T(8,128)(2,1)S(1)} copy-done((bf16[320,64,64]{0,2,1:T(8,128)(2,1)S(1)}, bf16[320,64,64]{0,2,1:T(8,128)(2,1)}, u32[]{:S(2)}) %copy-start.1) | copy-done | bytes 2621464
  114.5 0.0 copy-start.2
  114.5 1.6 %copy-done.2 = bf16[256,32,128]{2,0,1:T(8,128)(2,1)S(1)} copy-done((bf16[256,32,128]{2,0,1:T(8,128)(2,1)S(1)}, bf16[256,32,128]{2,0,1:T(8,128)(2,1)}, u32[]{:S(2)}) %copy-start.2) | copy-done | bytes 2097176
  116.1 6.1 %shard_map.80 = bf16[64,64,320]{2,1,0:T(8,128)(2,1)} custom-call(s32[256,1]{1,0:T(8,128)S(1)} %broadcast_subtract_fusion.place_ref, bf16[64,64,320]{2,1,0:T(8,128)(2,1)S(1)} %bitcast.39, bf16[32,256,128]{2,1,0:T(8,128)(2,1)S(1)} %bitcast.41), custom_call_target="tpu_custom_call" | custom-call | flops 671088640 | bytes 7340032 | tf_op jit(solution)/shard_map/pallas_call | solution.py:73
  122.2 0.0 copy-start.4
  122.2 13.1 %all-to-all-done.1 = bf16[128,32,128]{2,1,0:T(8,128)(2,1)} async-done(((bf16[128,32,128]{2,1,0:T(8,128)(2,1)}), bf16[128,32,128]{2,1,0:T(8,128)(2,1)}, u32[]{:S(2)}, u32[]{:S(2)}) %all-to-all-start.1) | async-done | bytes 1048608 | tf_op jit(solution)/shard_map/all_to_all | solution.py:312
  135.3 1.9 %gather_fusion.2 = bf16[64,32,128]{2,1,0:T(8,128)(2,1)S(1)} fusion(bf16[128,32,128]{2,1,0:T(8,128)(2,1)} %all-to-all-done.1, s32[1024]{0:T(1024)S(1)} %pad_clamp_fusion.1), kind=kCustom, calls=%fused_computation.2 | custom fusion | bytes 1048832 | tf_op jit(solution)/shard_map/gather | solution.py:316
  137.2 0.2 fusion.30
  137.4 0.0 copy-done.4
  137.4 1.5 %fusion.4 = bf16[64,128,64]{1,2,0:T(8,128)(2,1)} fusion(bf16[64,128,64]{1,2,0:T(8,128)(2,1)S(1)} %copy-done.4, bf16[64,32,64]{2,1,0:T(8,128)(2,1)S(1)} %get-tuple-element.15, bf16[64,32,64]{2,1,0:T(8,128)(2,1)S(1)} %get-tuple-element.14), kind=kOutput, calls=%fused_computation.14 | convolution fusion | flops 68681728 | bytes 2621440 | tf_op jit(solution)/shard_map/sea,sab->seb/dot_general | solution.py:315
  (13 shorter events, 0.1 us)
Async XLA Ops:
  2.3 10.9 %all-to-all-start = ((s32[32,1,8]{2,1,0:T(1,128)}), s32[32,1,8]{2,1,0:T(1,128)S(1)}, u32[]{:S(2)}, u32[]{:S(2)}) async-start(s32[32,1,8]{2,1,0:T(1,128)} %bitcast), calls=%async_computation | async-start | bytes 32768 | tf_op jit(solution)/shard_map/all_to_all | solution.py:281
  14.7 1.9 %copy-start = (bf16[320,64,64]{0,2,1:T(8,128)(2,1)S(1)}, bf16[320,64,64]{0,2,1:T(8,128)(2,1)}, u32[]{:S(2)}) copy-start(bf16[320,64,64]{0,2,1:T(8,128)(2,1)} %param.9) | copy-start | bytes 7864324
  58.8 1.2 copy-start.3
  58.8 1.5 %copy-start.5 = (bf16[64,128,64]{1,2,0:T(8,128)(2,1)S(1)}, bf16[64,128,64]{1,2,0:T(8,128)(2,1)}, u32[]{:S(2)}) copy-start(bf16[64,128,64]{1,2,0:T(8,128)(2,1)} %param.7) | copy-start | bytes 3145732
  59.0 1.9 %copy-start.6 = (bf16[64,128]{1,0:T(8,128)(2,1)S(1)}, bf16[64,128]{1,0:T(8,128)(2,1)}, u32[]{:S(2)}) copy-start(bf16[64,128]{1,0:T(8,128)(2,1)} %param.8) | copy-start | bytes 49156
  59.0 1.9 %copy-start.7 = (s32[64]{0:T(128)S(1)}, s32[64]{0:T(128)}, u32[]{:S(2)}) copy-start(s32[64]{0:T(128)} %param.11) | copy-start | bytes 772
  99.6 35.7 %all-to-all-start.1 = ((bf16[128,32,128]{2,1,0:T(8,128)(2,1)}), bf16[128,32,128]{2,1,0:T(8,128)(2,1)}, u32[]{:S(2)}, u32[]{:S(2)}) async-start(bf16[128,32,128]{2,1,0:T(8,128)(2,1)} %fusion.1), calls=%async_computation.1 | async-start | bytes 2097152 | tf_op jit(solution)/shard_map/all_to_all | solution.py:312
  112.6 1.9 %copy-start.1 = (bf16[320,64,64]{0,2,1:T(8,128)(2,1)S(1)}, bf16[320,64,64]{0,2,1:T(8,128)(2,1)}, u32[]{:S(2)}) copy-start(bf16[320,64,64]{0,2,1:T(8,128)(2,1)} %param.9) | copy-start | bytes 7864324
  114.5 1.6 %copy-start.2 = (bf16[256,32,128]{2,0,1:T(8,128)(2,1)S(1)}, bf16[256,32,128]{2,0,1:T(8,128)(2,1)}, u32[]{:S(2)}) copy-start(bf16[256,32,128]{2,0,1:T(8,128)(2,1)} %copy.58) | copy-start | bytes 6291460
  122.2 15.2 %copy-start.4 = (bf16[64,128,64]{1,2,0:T(8,128)(2,1)S(1)}, bf16[64,128,64]{1,2,0:T(8,128)(2,1)}, u32[]{:S(2)}) copy-start(bf16[64,128,64]{1,2,0:T(8,128)(2,1)} %param.6) | copy-start | bytes 3145732

commit v5 on v4

--- a/solution.py
+++ b/solution.py
@@ -50,39 +50,8 @@
     )(places, core_t)
 
 
-def apply_kernel(place_ref, core_ref, grads_ref, out_ref):
-    half = grads_ref.shape[0]
-    rank = out_ref.shape[1]
-    hot = one_hot(place_ref[...], core_ref.shape[2])
-
-    def step(i, carry):
-        total = lax.dot_general(
-            grads_ref[i], hot, (((0,), (0,)), ((), ())), preferred_element_type=jnp.float32
-        )
-        for part, row in ((0, i), (1, i + half)):
-            change = total[part * rank:(part + 1) * rank]
-            out_ref[row] = (core_ref[row].astype(jnp.float32) - change).astype(out_ref.dtype)
-        return carry
-
-    lax.fori_loop(0, half, step, 0, unroll=2)
-
-
-def apply_grads(core_t, grads, places):
-    rank, _, count = core_t.shape
-    wanted = places.shape[0]
-    return pl.pallas_call(
-        apply_kernel,
-        out_shape=jax.ShapeDtypeStruct(core_t.shape, core_t.dtype),
-        compiler_params=pltpu.CompilerParams(vmem_limit_bytes=48 * 2**20),
-        cost_estimate=pl.CostEstimate(
-            flops=2 * wanted * count * rank * rank,
-            bytes_accessed=2 * rank * rank * (2 * count + wanted),
-            transcendentals=0,
-        ),
-    )(places, core_t, grads)
-
-
 MESH = pl.DeviceIdType.MESH
+LANES = 128
 
 
 def greet(groups, owners):
@@ -260,6 +229,117 @@
     )(send)
 
 
+def swap_kernel(groups, owners, want, out, send_sem, recv_sem):
+    grp, own = lax.axis_index("grp"), lax.axis_index("own")
+    everyone = groups * owners
+    me = grp * owners + own
+    barrier = pltpu.get_barrier_semaphore()
+
+    def peer(i):
+        other = lax.rem(me + i + 1, everyone)
+        return other // owners, lax.rem(other, owners)
+
+    def hail(i, carry):
+        pl.semaphore_signal(barrier, inc=1, device_id=peer(i), device_id_type=MESH)
+        return carry
+
+    def copy(i):
+        to = peer(i)
+        return pltpu.make_async_remote_copy(
+            src_ref=want.at[to[1]],
+            dst_ref=out.at[me],
+            send_sem=send_sem.at[i],
+            recv_sem=recv_sem.at[i],
+            device_id=to,
+            device_id_type=MESH,
+        )
+
+    def launch(i, carry):
+        copy(i).start()
+        return carry
+
+    def drain(i, carry):
+        copy(i).wait()
+        return carry
+
+    lax.fori_loop(0, everyone - 1, hail, 0)
+    pl.semaphore_wait(barrier, everyone - 1)
+    lax.fori_loop(0, everyone - 1, launch, 0)
+    out[me] = want[own]
+    lax.fori_loop(0, everyone - 1, drain, 0)
+
+
+def swap(want, groups, owners):
+    everyone = groups * owners
+    return pl.pallas_call(
+        functools.partial(swap_kernel, groups, owners),
+        out_shape=jax.ShapeDtypeStruct((everyone,) + want.shape[1:], want.dtype),
+        in_specs=[pl.BlockSpec(memory_space=pltpu.VMEM)],
+        out_specs=pl.BlockSpec(memory_space=pltpu.VMEM),
+        scratch_shapes=[pltpu.SemaphoreType.DMA((everyone - 1,)), pltpu.SemaphoreType.DMA((everyone - 1,))],
+        compiler_params=pltpu.CompilerParams(collective_id=3, has_side_effects=True),
+    )(want)
+
+
+def finish_kernel(owners, place_ref, core_ref, grads_ref, fresh, out_ref, back, send_sem, recv_sem):
+    grp, own = lax.axis_index("grp"), lax.axis_index("own")
+    cap = fresh.shape[0] // owners
+    half = grads_ref.shape[0]
+    rank = out_ref.shape[1]
+    greet(1, owners)
+
+    def along(i):
+        peer = lax.rem(own + i + 1, owners)
+        return pltpu.make_async_remote_copy(
+            src_ref=fresh.at[pl.ds(peer * cap, cap)],
+            dst_ref=back.at[pl.ds(own * cap, cap)],
+            send_sem=send_sem.at[i],
+            recv_sem=recv_sem.at[i],
+            device_id=(grp, peer),
+            device_id_type=MESH,
+        )
+
+    def launch(i, carry):
+        along(i).start()
+        return carry
+
+    def drain(i, carry):
+        along(i).wait()
+        return carry
+
+    lax.fori_loop(0, owners - 1, launch, 0)
+    back[pl.ds(own * cap, cap)] = fresh[pl.ds(own * cap, cap)]
+    hot = one_hot(place_ref[...], core_ref.shape[2])
+
+    def step(i, carry):
+        total = lax.dot_general(
+            grads_ref[i], hot, (((0,), (0,)), ((), ())), preferred_element_type=jnp.float32
+        )
+        for part, row in ((0, i), (1, i + half)):
+            change = total[part * rank:(part + 1) * rank]
+            out_ref[row] = (core_ref[row].astype(jnp.float32) - change).astype(out_ref.dtype)
+        return carry
+
+    lax.fori_loop(0, half, step, 0)
+    lax.fori_loop(0, owners - 1, drain, 0)
+
+
+def finish(core_t, grads, places, fresh, owners):
+    return pl.pallas_call(
+        functools.partial(finish_kernel, owners),
+        out_shape=[
+            jax.ShapeDtypeStruct(core_t.shape, core_t.dtype),
+            jax.ShapeDtypeStruct(fresh.shape, fresh.dtype),
+        ],
+        in_specs=[pl.BlockSpec(memory_space=pltpu.VMEM)] * 4,
+        out_specs=[pl.BlockSpec(memory_space=pltpu.VMEM)] * 2,
+        scratch_shapes=[pltpu.SemaphoreType.DMA((owners - 1,)), pltpu.SemaphoreType.DMA((owners - 1,))],
+        compiler_params=pltpu.CompilerParams(
+            collective_id=4, has_side_effects=True, vmem_limit_bytes=48 * 2**20
+        ),
+    )(places, core_t, grads, fresh)
+
+
 def body(left, right, values, core, tile_slice, tile_fill):
     owners = lax.axis_size("own")
     groups = lax.axis_size("grp")
@@ -278,10 +358,8 @@
     live = jnp.any(match, axis=1)
     tile_of_slot = jnp.sum(jnp.where(match, pos[None, :], 0), axis=1)
     want = jnp.sum(jnp.where(match, place[None, :] + 1, 0), axis=1) - 1
-    table = lax.all_to_all(
-        jnp.broadcast_to(want.reshape(1, owners, cap), (groups, owners, cap)).reshape(groups * owners, cap),
-        ("grp", "own"), split_axis=0, concat_axis=0, tiled=True,
-    ).reshape(groups, slots)
+    wide = jnp.broadcast_to(want.reshape(owners, cap, 1), (owners, cap, LANES))
+    table = swap(wide, groups, owners)[:, :, 0].reshape(groups, slots)
 
     def shifted(step):
         return (grp + step) % groups
@@ -309,8 +387,9 @@
     pick = (mine[:, None] == place_of[None, :]).astype(jnp.bfloat16)
     total = jnp.einsum("st,tab->sab", pick, flat, preferred_element_type=jnp.float32)
     fresh = (old.astype(jnp.float32) - total).astype(jnp.bfloat16)
-    back = lax.all_to_all(fresh, "own", split_axis=0, concat_axis=0, tiled=True)
-    new_core_t = apply_grads(core_t, jnp.transpose(flat, (1, 0, 2)), (place_of - grp * per_device)[:, None])
+    new_core_t, back = finish(
+        core_t, jnp.transpose(flat, (1, 0, 2)), (place_of - grp * per_device)[:, None], fresh, owners
+    )
     new_core = jnp.transpose(new_core_t, (2, 0, 1))
     new_left = jnp.einsum(
         "sea,sab->seb", left, unpack(back[slot_of_tile]), preferred_element_type=jnp.float32

time: 140 us -> 142 us (1.014)
  Pallas kernels: 79.5 us -> 121 us
  waiting for transfers between devices: 17.6 us -> 0 us
  starting transfers between devices: 17 us -> 0 us
  local copies, waits for them, and re-layouts: 15.5 us -> 12.9 us
  other arithmetic: 4.65 us -> 3 us
    pallas_call x1 -> x2, Pallas kernels: 6.05 us -> 47.6 us  [the longest x1 36.5 us: finish(): pl.pallas_call(functools.partial(finish_kernel, owners), out_shape=[jax.S...]
    all_to_all x2 -> x0, waiting for transfers between devices: 17.6 us -> none  [the longest x1 13.1 us: body(): back = lax.all_to_all(fresh, 'own', split_axis=0, concat_axis=0, tiled=True)]
    all_to_all x2 -> x0, starting transfers between devices: 17 us -> none  [the longest x1 10.7 us: body(): back = lax.all_to_all(fresh, 'own', split_axis=0, concat_axis=0, tiled=True)]
    slice x0 -> x1, local copies, waits for them, and re-layouts: none -> 1.52 us  [body(): table = swap(wide, groups, owners)[:, :, 0].reshape(groups, slots)]
    unnamed x16 -> x15, local copies, waits for them, and re-layouts: 6.67 us -> 5.49 us
  transfers between devices with their start and end apart: 2 -> 0, of which waited for: 2 -> 0; matrix products, arithmetic and copies ran while one was open for 2% -> 0% of each run, Pallas kernels for 4% -> 0%
where the time goes in v5:
time: 142 us
  Pallas kernels  121 us (85%)
  local copies, waits for them, and re-layouts  12.9 us (9%)
  matrix products  3.66 us (3%)
  other arithmetic  3 us (2%)
    pallas_call x1, Pallas kernels, finish(): pl.pallas_call(functools.partial(finish_kernel, owners), out_shape=[jax.S...  36.5 us
    pallas_call x1, Pallas kernels, deliver(): pl.pallas_call(functools.partial(deliver_kernel, groups, owners), out_sha...  35.6 us
    pallas_call x1, Pallas kernels, collect(): pl.pallas_call(functools.partial(collect_kernel, groups, owners), out_sha...  33.4 us
    pallas_call x1, Pallas kernels, swap(): pl.pallas_call(functools.partial(swap_kernel, groups, owners), out_shape=...  11.1 us
    unnamed x15, local copies, waits for them, and re-layouts  5.49 us
    pallas_call x1, Pallas kernels, fetch(): pl.pallas_call(fetch_kernel, out_shape=jax.ShapeDtypeStruct((rank // 2, w...  4.41 us

profile of v5, /device:TPU:13, one launch (start us, length us, event | category | flops | bytes accessed | tf_op | source)
XLA Modules:
  0.0 141.5 jit_solution(9173420674704761715)
XLA Ops:
  0.7 0.7 fusion.22
  1.4 0.2 convert_reduce_fusion
  1.6 0.1 fusion.16
  1.7 0.1 select_reduce_fusion
  1.8 0.1 sub.44
  1.9 0.7 broadcast_in_dim.63.want
  2.6 11.1 %shard_map.77 = s32[32,8,128]{2,1,0:T(8,128)} custom-call(s32[16,8,128]{2,1,0:T(8,128)} %broadcast_in_dim.63.want), custom_call_target="tpu_custom_call" | custom-call | tf_op jit(solution)/shard_map/pallas_call | solution.py:274
  13.7 1.5 %slice_reduce_fusion = s32[32,8]{1,0:T(8,128)S(1)} fusion(s32[32,8,128]{2,1,0:T(8,128)} %shard_map.77), kind=kLoop, calls=%fused_computation.24 | loop fusion | bytes 2048 | tf_op jit(solution)/shard_map/slice | solution.py:362
  15.2 0.1 reshape_squeeze.3
  15.4 0.1 copy.39
  15.6 0.1 copy.41.place_ref
  15.7 0.0 copy-start
  15.7 1.9 %copy-done = bf16[320,64,64]{0,2,1:T(8,128)(2,1)S(1)} copy-done((bf16[320,64,64]{0,2,1:T(8,128)(2,1)S(1)}, bf16[320,64,64]{0,2,1:T(8,128)(2,1)}, u32[]{:S(2)}) %copy-start) | copy-done | bytes 2621464
  17.6 4.4 %shard_map.78 = bf16[32,256,128]{2,1,0:T(8,128)(2,1)S(1)} custom-call(s32[256,1]{1,0:T(8,128)S(1)} %copy.41.place_ref, bf16[64,64,320]{2,1,0:T(8,128)(2,1)S(1)} %bitcast.38), custom_call_target="tpu_custom_call" | custom-call | flops 671088640 | bytes 4718592 | tf_op jit(solution)/shard_map/pallas_call | solution.py:43
  22.0 1.4 copy.57
  23.4 35.6 %shard_map.79 = (bf16[128,32,128]{2,1,0:T(8,128)(2,1)S(1)}, bf16[128,32,128]{2,1,0:T(8,128)(2,1)S(1)}) custom-call(bf16[256,32,128]{2,1,0:T(8,128)(2,1)S(1)} %bitcast.40), custom_call_target="tpu_custom_call" | custom-call | tf_op jit(solution)/shard_map/pallas_call | solution.py:137
  59.0 0.7 gather_fusion
  59.6 0.0 copy-start.1
  59.6 0.0 copy-start.4
  59.7 0.2 fusion.31
  59.9 0.0 copy-start.5
  59.9 0.0 copy-start.6
  59.9 1.0 copy-done.1
  60.9 0.3 copy-done.4
  61.2 0.6 fusion
  61.8 0.0 copy-done.5
  61.8 0.0 copy-done.6
  61.8 0.1 subtract_select_fusion
  61.9 0.7 convolution_convert_fusion.1
  62.6 0.1 fusion.29
  62.7 0.3 pad_maximum_fusion
  63.0 0.8 gather_fusion.1
  63.7 0.2 broadcast_select_fusion.send
  63.9 33.4 %shard_map.80 = bf16[256,32,128]{2,1,0:T(8,128)(2,1)S(1)} custom-call(bf16[128,32,128]{2,1,0:T(8,128)(2,1)S(1)} %broadcast_select_fusion.send), custom_call_target="tpu_custom_call" | custom-call | tf_op jit(solution)/shard_map/pallas_call | solution.py:215
  97.4 0.9 fusion.2
  98.2 1.3 fusion.1.fresh
  99.5 0.8 copy.58
  100.3 36.5 %shard_map.81 = (bf16[64,64,320]{2,1,0:T(8,128)(2,1)}, bf16[128,32,128]{2,1,0:T(8,128)(2,1)S(1)}) custom-call(s32[256,1]{1,0:T(8,128)S(1)} %broadcast_subtract_fusion.place_ref, bf16[64,64,320]{2,1,0:T(8,128)(2,1)} %bitcast.37, bf16[32,256,128]{2,1,0:T(8,128)(2,1)S(1)} %bitcast.39, bf16[128,32,128]{2,1,0:T(8,128)(2,1)S(1)} %fusion.1.fresh), custom_call_target="tpu_custom_call" | custom-call | tf_op jit(solution)/shard_map/pallas_call | solution.py:328
  136.9 0.0 copy-start.2
  136.9 0.7 gather_fusion.2
  137.5 0.2 fusion.30
  137.7 0.0 copy-start.3
  137.8 0.3 copy-done.2
  138.1 1.5 %fusion.4 = bf16[64,128,64]{1,2,0:T(8,128)(2,1)} fusion(bf16[64,128,64]{1,2,0:T(8,128)(2,1)S(1)} %copy-done.2, bf16[64,32,64]{2,1,0:T(8,128)(2,1)S(1)} %get-tuple-element.19, bf16[64,32,64]{2,1,0:T(8,128)(2,1)S(1)} %get-tuple-element.18), kind=kOutput, calls=%fused_computation.14 | convolution fusion | flops 68681728 | bytes 2621440 | tf_op jit(solution)/shard_map/sea,sab->seb/dot_general | solution.py:394
  139.6 0.3 copy-done.3
  139.9 1.7 %copy.60 = bf16[320,64,64]{0,2,1:T(8,128)(2,1)} copy(bf16[320,64,64]{0,2,1:T(8,128)(2,1)S(1)} %bitcast.41) | data formatting | bytes 5242880
  (13 shorter events, 0.1 us)
Async XLA Ops:
  15.7 1.9 %copy-start = (bf16[320,64,64]{0,2,1:T(8,128)(2,1)S(1)}, bf16[320,64,64]{0,2,1:T(8,128)(2,1)}, u32[]{:S(2)}) copy-start(bf16[320,64,64]{0,2,1:T(8,128)(2,1)} %param.9) | copy-start | bytes 7864324
  59.6 1.2 copy-start.1
  59.6 1.5 %copy-start.4 = (bf16[64,128,64]{1,2,0:T(8,128)(2,1)S(1)}, bf16[64,128,64]{1,2,0:T(8,128)(2,1)}, u32[]{:S(2)}) copy-start(bf16[64,128,64]{1,2,0:T(8,128)(2,1)} %param.7) | copy-start | bytes 3145732
  59.9 1.9 %copy-start.5 = (bf16[64,128]{1,0:T(8,128)(2,1)S(1)}, bf16[64,128]{1,0:T(8,128)(2,1)}, u32[]{:S(2)}) copy-start(bf16[64,128]{1,0:T(8,128)(2,1)} %param.8) | copy-start | bytes 49156
  59.9 1.9 %copy-start.6 = (s32[64]{0:T(128)S(1)}, s32[64]{0:T(128)}, u32[]{:S(2)}) copy-start(s32[64]{0:T(128)} %param.11) | copy-start | bytes 772
  136.9 1.2 copy-start.2
  137.7 2.1 %copy-start.3 = (bf16[64,64,320]{2,1,0:T(8,128)(2,1)S(1)}, bf16[64,64,320]{2,1,0:T(8,128)(2,1)}, u32[]{:S(2)}) copy-start(bf16[64,64,320]{2,1,0:T(8,128)(2,1)} %get-tuple-element.8) | copy-start | bytes 7864324

commit v6 on v5

--- a/solution.py
+++ b/solution.py
@@ -54,6 +54,16 @@
 LANES = 128
 
 
+def route(own, i, owners):
+    if owners % 2:
+        return lax.rem(own + i + 1, owners), lax.rem(own - i - 1 + owners, owners)
+    half = owners // 2
+    near = i // half
+    base = lax.rem(own // half + 1 - near, 2) * half
+    place = lax.rem(own, half)
+    return base + lax.rem(place + i + near, half), base + lax.rem(place - i - near + owners, half)
+
+
 def greet(groups, owners):
     grp, own = lax.axis_index("grp"), lax.axis_index("own")
     barrier = pltpu.get_barrier_semaphore()
@@ -75,7 +85,7 @@
     greet(groups, owners)
 
     def cross(step, i):
-        start = lax.rem(own + i + 1, owners) * cap
+        start = route(own, i, owners)[0] * cap
         return pltpu.make_async_remote_copy(
             src_ref=rows.at[pl.ds(step * slots + start, cap)],
             dst_ref=inbox.at[step - 1, pl.ds(start, cap)],
@@ -86,7 +96,7 @@
         )
 
     def along(i):
-        peer = lax.rem(own + i + 1, owners)
+        peer = route(own, i, owners)[0]
         return pltpu.make_async_remote_copy(
             src_ref=old.at[pl.ds(peer * cap, cap)],
             dst_ref=out.at[pl.ds(own * cap, cap)],
@@ -102,7 +112,7 @@
         return carry
 
     def merge(i):
-        start = lax.rem(own + i + 1, owners) * cap
+        start = route(own, i, owners)[0] * cap
         total = rows[pl.ds(start, cap)]
         for step in range(1, groups):
             cross(step, i).wait_recv()
@@ -158,8 +168,11 @@
     cap = slots // owners
     greet(groups, owners)
 
+    def turn(i):
+        return i if owners % 2 else i // 2 + i % 2 * (owners // 2)
+
     def along(i):
-        peer = lax.rem(own + i + 1, owners)
+        peer = route(own, turn(i), owners)[0]
         return pltpu.make_async_remote_copy(
             src_ref=send.at[pl.ds(peer * cap, cap)],
             dst_ref=flat.at[pl.ds(own * cap, cap)],
@@ -170,7 +183,7 @@
         )
 
     def cross(step, i):
-        start = lax.rem(own - i - 1 + owners, owners) * cap
+        start = route(own, turn(i), owners)[1] * cap
         return pltpu.make_async_remote_copy(
             src_ref=flat.at[pl.ds(start, cap)],
             dst_ref=flat.at[pl.ds(step * slots + start, cap)],
@@ -289,7 +302,7 @@
     greet(1, owners)
 
     def along(i):
-        peer = lax.rem(own + i + 1, owners)
+        peer = route(own, i, owners)[0]
         return pltpu.make_async_remote_copy(
             src_ref=fresh.at[pl.ds(peer * cap, cap)],
             dst_ref=back.at[pl.ds(own * cap, cap)],

time: 142 us -> 135 us (0.951); the launches traced: 142 us -> 132 us
  Pallas kernels: 121 us -> 112 us
    pallas_call x1, Pallas kernels: 36.5 us -> 31.9 us  [finish(): pl.pallas_call(functools.partial(finish_kernel, owners), out_shape=[jax.S...]
    pallas_call x1, Pallas kernels: 35.6 us -> 32.2 us  [deliver(): pl.pallas_call(functools.partial(deliver_kernel, groups, owners), out_sha...]
where the time goes in v6:
time: 135 us; the launch traced here: 132 us
  Pallas kernels  112 us (83%)
  local copies, waits for them, and re-layouts  12.9 us (10%)
  matrix products  3.66 us (3%)
  other arithmetic  3 us (2%)
    pallas_call x1, Pallas kernels, collect(): pl.pallas_call(functools.partial(collect_kernel, groups, owners), out_sha...  32.2 us
    pallas_call x1, Pallas kernels, deliver(): pl.pallas_call(functools.partial(deliver_kernel, groups, owners), out_sha...  32.2 us
    pallas_call x1, Pallas kernels, finish(): pl.pallas_call(functools.partial(finish_kernel, owners), out_shape=[jax.S...  31.9 us
    pallas_call x1, Pallas kernels, swap(): pl.pallas_call(functools.partial(swap_kernel, groups, owners), out_shape=...  11.1 us
    unnamed x15, local copies, waits for them, and re-layouts  5.49 us
    pallas_call x1, Pallas kernels, fetch(): pl.pallas_call(fetch_kernel, out_shape=jax.ShapeDtypeStruct((rank // 2, w...  4.41 us

profile of v6, /device:TPU:13, one launch (start us, length us, event | category | flops | bytes accessed | tf_op | source)
XLA Modules:
  0.0 132.3 jit_solution(13014051593749896810)
XLA Ops:
  0.7 0.7 fusion.22
  1.4 0.2 convert_reduce_fusion
  1.6 0.1 fusion.16
  1.7 0.1 select_reduce_fusion
  1.8 0.1 sub.44
  1.9 0.7 broadcast_in_dim.63.want
  2.6 11.1 %shard_map.77 = s32[32,8,128]{2,1,0:T(8,128)} custom-call(s32[16,8,128]{2,1,0:T(8,128)} %broadcast_in_dim.63.want), custom_call_target="tpu_custom_call" | custom-call | tf_op jit(solution)/shard_map/pallas_call | solution.py:287
  13.7 1.5 %slice_reduce_fusion = s32[32,8]{1,0:T(8,128)S(1)} fusion(s32[32,8,128]{2,1,0:T(8,128)} %shard_map.77), kind=kLoop, calls=%fused_computation.24 | loop fusion | bytes 2048 | tf_op jit(solution)/shard_map/slice | solution.py:375
  15.2 0.1 reshape_squeeze.3
  15.4 0.1 copy.39
  15.6 0.1 copy.41.place_ref
  15.7 0.0 copy-start
  15.7 1.9 %copy-done = bf16[320,64,64]{0,2,1:T(8,128)(2,1)S(1)} copy-done((bf16[320,64,64]{0,2,1:T(8,128)(2,1)S(1)}, bf16[320,64,64]{0,2,1:T(8,128)(2,1)}, u32[]{:S(2)}) %copy-start) | copy-done | bytes 2621464
  17.6 4.4 %shard_map.78 = bf16[32,256,128]{2,1,0:T(8,128)(2,1)S(1)} custom-call(s32[256,1]{1,0:T(8,128)S(1)} %copy.41.place_ref, bf16[64,64,320]{2,1,0:T(8,128)(2,1)S(1)} %bitcast.38), custom_call_target="tpu_custom_call" | custom-call | flops 671088640 | bytes 4718592 | tf_op jit(solution)/shard_map/pallas_call | solution.py:43
  22.0 1.4 %copy.57 = bf16[32,256,128]{2,0,1:T(8,128)(2,1)S(1)} copy(bf16[32,256,128]{2,1,0:T(8,128)(2,1)S(1)} %shard_map.78) | data formatting | bytes 4194304 | tf_op jit(solution)/shard_map/pallas_call | solution.py:43
  23.4 32.2 %shard_map.79 = (bf16[128,32,128]{2,1,0:T(8,128)(2,1)S(1)}, bf16[128,32,128]{2,1,0:T(8,128)(2,1)S(1)}) custom-call(bf16[256,32,128]{2,1,0:T(8,128)(2,1)S(1)} %bitcast.40), custom_call_target="tpu_custom_call" | custom-call | tf_op jit(solution)/shard_map/pallas_call | solution.py:147
  55.6 0.7 gather_fusion
  56.2 0.0 copy-start.1
  56.2 0.0 copy-start.4
  56.3 0.2 fusion.31
  56.5 0.0 copy-start.5
  56.5 0.0 copy-start.6
  56.5 1.0 copy-done.1
  57.5 0.3 copy-done.4
  57.8 0.6 fusion
  58.4 0.0 copy-done.5
  58.4 0.0 copy-done.6
  58.4 0.1 subtract_select_fusion
  58.5 0.7 convolution_convert_fusion.1
  59.2 0.1 fusion.29
  59.3 0.3 pad_maximum_fusion
  59.6 0.8 gather_fusion.1
  60.3 0.2 broadcast_select_fusion.send
  60.5 32.2 %shard_map.80 = bf16[256,32,128]{2,1,0:T(8,128)(2,1)S(1)} custom-call(bf16[128,32,128]{2,1,0:T(8,128)(2,1)S(1)} %broadcast_select_fusion.send), custom_call_target="tpu_custom_call" | custom-call | tf_op jit(solution)/shard_map/pallas_call | solution.py:228
  92.8 0.9 fusion.2
  93.7 1.3 fusion.1.fresh
  95.0 0.8 copy.58
  95.8 31.9 %shard_map.81 = (bf16[64,64,320]{2,1,0:T(8,128)(2,1)}, bf16[128,32,128]{2,1,0:T(8,128)(2,1)S(1)}) custom-call(s32[256,1]{1,0:T(8,128)S(1)} %broadcast_subtract_fusion.place_ref, bf16[64,64,320]{2,1,0:T(8,128)(2,1)} %bitcast.37, bf16[32,256,128]{2,1,0:T(8,128)(2,1)S(1)} %bitcast.39, bf16[128,32,128]{2,1,0:T(8,128)(2,1)S(1)} %fusion.1.fresh), custom_call_target="tpu_custom_call" | custom-call | tf_op jit(solution)/shard_map/pallas_call | solution.py:341
  127.6 0.0 copy-start.2
  127.7 0.7 gather_fusion.2
  128.3 0.2 fusion.30
  128.5 0.0 copy-start.3
  128.5 0.3 copy-done.2
  128.9 1.5 %fusion.4 = bf16[64,128,64]{1,2,0:T(8,128)(2,1)} fusion(bf16[64,128,64]{1,2,0:T(8,128)(2,1)S(1)} %copy-done.2, bf16[64,32,64]{2,1,0:T(8,128)(2,1)S(1)} %get-tuple-element.19, bf16[64,32,64]{2,1,0:T(8,128)(2,1)S(1)} %get-tuple-element.18), kind=kOutput, calls=%fused_computation.14 | convolution fusion | flops 68681728 | bytes 2621440 | tf_op jit(solution)/shard_map/sea,sab->seb/dot_general | solution.py:407
  130.4 0.3 copy-done.3
  130.7 1.7 %copy.60 = bf16[320,64,64]{0,2,1:T(8,128)(2,1)} copy(bf16[320,64,64]{0,2,1:T(8,128)(2,1)S(1)} %bitcast.41) | data formatting | bytes 5242880
  (13 shorter events, 0.1 us)
Async XLA Ops:
  15.7 1.9 %copy-start = (bf16[320,64,64]{0,2,1:T(8,128)(2,1)S(1)}, bf16[320,64,64]{0,2,1:T(8,128)(2,1)}, u32[]{:S(2)}) copy-start(bf16[320,64,64]{0,2,1:T(8,128)(2,1)} %param.9) | copy-start | bytes 7864324
  56.2 1.2 copy-start.1
  56.2 1.5 %copy-start.4 = (bf16[64,128,64]{1,2,0:T(8,128)(2,1)S(1)}, bf16[64,128,64]{1,2,0:T(8,128)(2,1)}, u32[]{:S(2)}) copy-start(bf16[64,128,64]{1,2,0:T(8,128)(2,1)} %param.7) | copy-start | bytes 3145732
  56.5 1.9 %copy-start.5 = (bf16[64,128]{1,0:T(8,128)(2,1)S(1)}, bf16[64,128]{1,0:T(8,128)(2,1)}, u32[]{:S(2)}) copy-start(bf16[64,128]{1,0:T(8,128)(2,1)} %param.8) | copy-start | bytes 49156
  56.5 1.9 %copy-start.6 = (s32[64]{0:T(128)S(1)}, s32[64]{0:T(128)}, u32[]{:S(2)}) copy-start(s32[64]{0:T(128)} %param.11) | copy-start | bytes 772
  127.6 1.2 copy-start.2
  128.5 2.1 %copy-start.3 = (bf16[64,64,320]{2,1,0:T(8,128)(2,1)S(1)}, bf16[64,64,320]{2,1,0:T(8,128)(2,1)}, u32[]{:S(2)}) copy-start(bf16[64,64,320]{2,1,0:T(8,128)(2,1)} %get-tuple-element.8) | copy-start | bytes 7864324

commit v7 on v6

--- a/solution.py
+++ b/solution.py
@@ -27,14 +27,21 @@
     half = out_ref.shape[0]
     hot = one_hot(place_ref[...], core_ref.shape[2])
 
+    rank = core_ref.shape[1]
+
     def step(i, carry):
-        slab = jnp.concatenate([core_ref[i], core_ref[i + half]], axis=0)
-        out_ref[i] = lax.dot_general(
+        row = 2 * i
+        slab = jnp.concatenate(
+            [core_ref[row], core_ref[row + half], core_ref[row + 1], core_ref[row + 1 + half]], axis=0
+        )
+        both = lax.dot_general(
             hot, slab, (((1,), (1,)), ((), ())), preferred_element_type=jnp.float32
         ).astype(out_ref.dtype)
-        return carry
-
-    lax.fori_loop(0, half, step, 0, unroll=2)
+        out_ref[row] = both[:, :2 * rank]
+        out_ref[row + 1] = both[:, 2 * rank:]
+        return carry
+
+    lax.fori_loop(0, half // 2, step, 0, unroll=2)
 
 
 def fetch(core_t, places):
@@ -371,8 +378,8 @@
     live = jnp.any(match, axis=1)
     tile_of_slot = jnp.sum(jnp.where(match, pos[None, :], 0), axis=1)
     want = jnp.sum(jnp.where(match, place[None, :] + 1, 0), axis=1) - 1
-    wide = jnp.broadcast_to(want.reshape(owners, cap, 1), (owners, cap, LANES))
-    table = swap(wide, groups, owners)[:, :, 0].reshape(groups, slots)
+    wide = jnp.pad(want.reshape(owners, 1, cap), ((0, 0), (0, 0), (0, LANES - cap)))
+    table = swap(wide, groups, owners)[:, 0, :cap].reshape(groups, slots)
 
     def shifted(step):
         return (grp + step) % groups

time: 135 us -> 131 us (0.970)
  Pallas kernels: 112 us -> 109 us
    pallas_call x1, Pallas kernels: 11.1 us -> 9.4 us  [swap(): pl.pallas_call(functools.partial(swap_kernel, groups, owners), out_shape=...]
    pallas_call x1, Pallas kernels: 4.41 us -> 2.77 us  [fetch(): pl.pallas_call(fetch_kernel, out_shape=jax.ShapeDtypeStruct((rank // 2, w...]
where the time goes in v7:
time: 131 us; the launch traced here: 128 us
  Pallas kernels  109 us (83%)
  local copies, waits for them, and re-layouts  12.1 us (9%)
  matrix products  3.65 us (3%)
  other arithmetic  3 us (2%)
    pallas_call x1, Pallas kernels, deliver(): pl.pallas_call(functools.partial(deliver_kernel, groups, owners), out_sha...  32.3 us
    pallas_call x1, Pallas kernels, collect(): pl.pallas_call(functools.partial(collect_kernel, groups, owners), out_sha...  32.2 us
    pallas_call x1, Pallas kernels, finish(): pl.pallas_call(functools.partial(finish_kernel, owners), out_shape=[jax.S...  31.9 us
    pallas_call x1, Pallas kernels, swap(): pl.pallas_call(functools.partial(swap_kernel, groups, owners), out_shape=...  9.4 us
    unnamed x15, local copies, waits for them, and re-layouts  5.49 us
    pallas_call x1, Pallas kernels, fetch(): pl.pallas_call(fetch_kernel, out_shape=jax.ShapeDtypeStruct((rank // 2, w...  2.77 us

profile of v7, /device:TPU:13, one launch (start us, length us, event | category | flops | bytes accessed | tf_op | source)
XLA Modules:
  0.0 128.3 jit_solution(14933656791671458006)
XLA Ops:
  0.7 0.7 fusion.22
  1.4 0.2 convert_reduce_fusion
  1.6 0.1 fusion.16
  1.7 0.1 select_reduce_fusion
  1.8 0.1 sub.44
  1.9 0.6 pad.4.want
  2.5 9.4 %shard_map.77 = s32[32,1,128]{2,1,0:T(1,128)} custom-call(s32[16,1,128]{2,1,0:T(1,128)} %pad.4.want), custom_call_target="tpu_custom_call" | custom-call | tf_op jit(solution)/shard_map/pallas_call | solution.py:294
  11.9 0.8 slice_reduce_fusion
  12.7 0.1 reshape_squeeze.3
  12.9 0.1 copy.44
  13.0 0.1 copy.46.place_ref
  13.2 0.0 copy-start
  13.2 1.9 %copy-done = bf16[320,64,64]{0,2,1:T(8,128)(2,1)S(1)} copy-done((bf16[320,64,64]{0,2,1:T(8,128)(2,1)S(1)}, bf16[320,64,64]{0,2,1:T(8,128)(2,1)}, u32[]{:S(2)}) %copy-start) | copy-done | bytes 2621464
  15.1 2.8 %shard_map.78 = bf16[32,256,128]{2,1,0:T(8,128)(2,1)S(1)} custom-call(s32[256,1]{1,0:T(8,128)S(1)} %copy.46.place_ref, bf16[64,64,320]{2,1,0:T(8,128)(2,1)S(1)} %bitcast.39), custom_call_target="tpu_custom_call" | custom-call | flops 671088640 | bytes 4718592 | tf_op jit(solution)/shard_map/pallas_call | solution.py:50
  17.8 1.4 %copy.62 = bf16[32,256,128]{2,0,1:T(8,128)(2,1)S(1)} copy(bf16[32,256,128]{2,1,0:T(8,128)(2,1)S(1)} %shard_map.78) | data formatting | bytes 4194304 | tf_op jit(solution)/shard_map/pallas_call | solution.py:50
  19.2 32.3 %shard_map.79 = (bf16[128,32,128]{2,1,0:T(8,128)(2,1)S(1)}, bf16[128,32,128]{2,1,0:T(8,128)(2,1)S(1)}) custom-call(bf16[256,32,128]{2,1,0:T(8,128)(2,1)S(1)} %bitcast.41), custom_call_target="tpu_custom_call" | custom-call | tf_op jit(solution)/shard_map/pallas_call | solution.py:154
  51.5 0.7 gather_fusion
  52.2 0.0 copy-start.1
  52.2 0.0 copy-start.4
  52.2 0.2 fusion.31
  52.5 0.0 copy-start.5
  52.5 0.0 copy-start.6
  52.5 1.0 copy-done.1
  53.4 0.3 copy-done.4
  53.8 0.6 fusion
  54.4 0.0 copy-done.5
  54.4 0.0 copy-done.6
  54.4 0.1 subtract_select_fusion
  54.5 0.7 convolution_convert_fusion.1
  55.2 0.1 fusion.29
  55.2 0.3 pad_maximum_fusion
  55.5 0.8 gather_fusion.1
  56.3 0.2 broadcast_select_fusion.send
  56.5 32.2 %shard_map.80 = bf16[256,32,128]{2,1,0:T(8,128)(2,1)S(1)} custom-call(bf16[128,32,128]{2,1,0:T(8,128)(2,1)S(1)} %broadcast_select_fusion.send), custom_call_target="tpu_custom_call" | custom-call | tf_op jit(solution)/shard_map/pallas_call | solution.py:235
  88.7 0.9 fusion.2
  89.6 1.3 %fusion.1.fresh = bf16[128,32,128]{2,1,0:T(8,128)(2,1)S(1)} fusion(f32[128,32,128]{2,0,1:T(8,128)S(1)} %fusion.2, bf16[128,32,128]{2,1,0:T(8,128)(2,1)S(1)} %get-tuple-element.7), kind=kLoop, calls=%fused_computation.6 | loop fusion | flops 1572864 | bytes 4194304 | tf_op jit(solution)/shard_map/convert_element_type | solution.py:409
  90.9 0.8 copy.63
  91.7 31.9 %shard_map.81 = (bf16[64,64,320]{2,1,0:T(8,128)(2,1)}, bf16[128,32,128]{2,1,0:T(8,128)(2,1)S(1)}) custom-call(s32[256,1]{1,0:T(8,128)S(1)} %broadcast_subtract_fusion.place_ref, bf16[64,64,320]{2,1,0:T(8,128)(2,1)} %bitcast.38, bf16[32,256,128]{2,1,0:T(8,128)(2,1)S(1)} %bitcast.40, bf16[128,32,128]{2,1,0:T(8,128)(2,1)S(1)} %fusion.1.fresh), custom_call_target="tpu_custom_call" | custom-call | tf_op jit(solution)/shard_map/pallas_call | solution.py:348
  123.6 0.0 copy-start.2
  123.6 0.7 gather_fusion.2
  124.3 0.2 fusion.30
  124.5 0.0 copy-start.3
  124.5 0.3 copy-done.2
  124.9 1.5 %fusion.4 = bf16[64,128,64]{1,2,0:T(8,128)(2,1)} fusion(bf16[64,128,64]{1,2,0:T(8,128)(2,1)S(1)} %copy-done.2, bf16[64,32,64]{2,1,0:T(8,128)(2,1)S(1)} %get-tuple-element.19, bf16[64,32,64]{2,1,0:T(8,128)(2,1)S(1)} %get-tuple-element.18), kind=kOutput, calls=%fused_computation.14 | convolution fusion | flops 68681728 | bytes 2621440 | tf_op jit(solution)/shard_map/sea,sab->seb/dot_general | solution.py:414
  126.4 0.3 copy-done.3
  126.7 1.7 %copy.65 = bf16[320,64,64]{0,2,1:T(8,128)(2,1)} copy(bf16[320,64,64]{0,2,1:T(8,128)(2,1)S(1)} %bitcast.42) | data formatting | bytes 5242880
  (13 shorter events, 0.1 us)
Async XLA Ops:
  13.2 1.9 %copy-start = (bf16[320,64,64]{0,2,1:T(8,128)(2,1)S(1)}, bf16[320,64,64]{0,2,1:T(8,128)(2,1)}, u32[]{:S(2)}) copy-start(bf16[320,64,64]{0,2,1:T(8,128)(2,1)} %param.9) | copy-start | bytes 7864324
  52.2 1.2 copy-start.1
  52.2 1.5 %copy-start.4 = (bf16[64,128,64]{1,2,0:T(8,128)(2,1)S(1)}, bf16[64,128,64]{1,2,0:T(8,128)(2,1)}, u32[]{:S(2)}) copy-start(bf16[64,128,64]{1,2,0:T(8,128)(2,1)} %param.7) | copy-start | bytes 3145732
  52.5 1.9 %copy-start.5 = (bf16[64,128]{1,0:T(8,128)(2,1)S(1)}, bf16[64,128]{1,0:T(8,128)(2,1)}, u32[]{:S(2)}) copy-start(bf16[64,128]{1,0:T(8,128)(2,1)} %param.8) | copy-start | bytes 49156
  52.5 1.9 %copy-start.6 = (s32[64]{0:T(128)S(1)}, s32[64]{0:T(128)}, u32[]{:S(2)}) copy-start(s32[64]{0:T(128)} %param.11) | copy-start | bytes 772
  123.6 1.2 copy-start.2
  124.5 2.1 %copy-start.3 = (bf16[64,64,320]{2,1,0:T(8,128)(2,1)S(1)}, bf16[64,64,320]{2,1,0:T(8,128)(2,1)}, u32[]{:S(2)}) copy-start(bf16[64,64,320]{2,1,0:T(8,128)(2,1)} %get-tuple-element.8) | copy-start | bytes 7864324
